TPU v7x, 32 devices: a whole 2x2x4 slice. The times are simulated.
32 devices in a mesh: seq: 8 (over y, x, core), tensor: 4 (over z).
Axes of the slice: x: 2, y: 2, z: 4, core: 2. Of those that a mesh axis runs over, the one named last changes fastest.
Arguments:
- tokens: bfloat16 [2048, 8192], P('seq', 'tensor'), may hold values from -24 to 24
- cotangent: bfloat16 [2048, 8192], P('seq', 'tensor'), may hold values from -6 to 6
- w_query: bfloat16 [8192, 4096], P(None, 'tensor'), may hold values from -1 to 1
- w_key: bfloat16 [8192, 1024], P(None, 'tensor'), may hold values from -1 to 1
- w_value: bfloat16 [8192, 1024], P(None, 'tensor'), may hold values from -0.0625 to 0.0625
- w_output: bfloat16 [4096, 8192], P('tensor'), may hold values from -0.09375 to 0.09375
- segments: int32 [2048], replicated, may hold values from 0 to 7, never falling along the last dimension, each value on 1 to 1024 neighbouring positions
- band: int32 [1], replicated, may hold values from 0 to 2047
Outputs:
- layer_out: bfloat16 [2048, 8192], P('seq', 'tensor')
- grad_tokens: bfloat16 [2048, 8192], P('seq', 'tensor')
- grad_query: float32 [8192, 4096], P('seq', 'tensor')
- grad_key: float32 [8192, 1024], P('seq', 'tensor')
- grad_value: float32 [8192, 1024], P('seq', 'tensor')
- grad_output: float32 [4096, 8192], P('tensor', 'seq')
All inputs are finite; a program needn't handle non-finite values.
Results may differ from a plain program's by a relative error of at most 0.025.
The roundings to bfloat16 on the way count: a program that leaves them out, or rounds other values in their place, can miss the bound.
Values may be sent and summed in bfloat16 or wider, within the bound.
A program may use at most 320 MiB of HBM per device.

v0:
```python
import math

import jax
import jax.numpy as jnp
from jax import lax
from jax.sharding import PartitionSpec as P

HD = 128


def tables(positions, width):
    half = width // 2
    freq = jnp.exp(-math.log(10000.0) * jnp.arange(half, dtype=jnp.float32) * 2.0 / width)
    angles = positions[:, None] * freq[None, :]
    return (jnp.cos(angles), jnp.sin(angles))


def rotate(values, cosine, sine, width):
    shaped = values.reshape(values.shape[0], -1, width)
    half = width // 2
    first = shaped[..., :half]
    second = shaped[..., half:]
    cos_b = cosine[:, None, :]
    sin_b = sine[:, None, :]
    turned = jnp.concatenate([first * cos_b - second * sin_b, second * cos_b + first * sin_b], -1)
    return turned.reshape(values.shape)


def rotate_back(values, cosine, sine, width):
    shaped = values.reshape(values.shape[0], -1, width)
    half = width // 2
    first = shaped[..., :half]
    second = shaped[..., half:]
    cos_b = cosine[:, None, :]
    sin_b = sine[:, None, :]
    turned = jnp.concatenate([first * cos_b + second * sin_b, second * cos_b - first * sin_b], -1)
    return turned.reshape(values.shape)


def contract_last(left, right):
    return lax.dot_general(
        left, right, (((1,), (1,)), ((), ())), preferred_element_type=jnp.float32
    )


def contract_first(left, right):
    return lax.dot_general(
        left, right, (((0,), (0,)), ((), ())), preferred_element_type=jnp.float32
    )


def on_device(tokens, cotangent, w_query, w_key, w_value, w_output, segments, band):
    f32 = jnp.float32
    bf16 = jnp.bfloat16
    factor = 1.0 / math.sqrt(HD)
    tok_rows = tokens.shape[0]
    seq_count = lax.axis_size("seq")
    all_rows = tok_rows * seq_count
    kv_local = w_key.shape[1] // HD
    group = w_query.shape[1] // w_key.shape[1]
    full_x, full_grad = (
        lax.all_gather(tokens, "tensor", axis=1, tiled=True),
        lax.all_gather(cotangent, "tensor", axis=1, tiled=True),
    )
    proj_q = jnp.dot(full_x, w_query, preferred_element_type=f32)
    proj_k = jnp.dot(full_x, w_key, preferred_element_type=f32)
    proj_v = jnp.dot(full_x, w_value, preferred_element_type=f32)
    first_row = lax.axis_index("seq") * tok_rows
    own_rows = first_row + jnp.arange(tok_rows)
    cosine, sine = tables(own_rows.astype(f32), HD)
    query = rotate(proj_q, cosine, sine, HD).astype(bf16)
    keys_local = rotate(proj_k, cosine, sine, HD).astype(bf16)
    values_local = proj_v.astype(bf16)
    keys, values = (
        lax.all_gather(keys_local, "seq", axis=0, tiled=True),
        lax.all_gather(values_local, "seq", axis=0, tiled=True),
    )
    key_rows = jnp.arange(all_rows)
    own_seg = lax.dynamic_slice_in_dim(segments, first_row, tok_rows)
    allowed = (own_seg[:, None] == segments[None, :]) & (
        key_rows[None, :] <= own_rows[:, None] + band[0]
    )
    query4 = query.reshape(tok_rows, kv_local, group, HD)
    keys3 = keys.reshape(all_rows, kv_local, HD)
    values3 = values.reshape(all_rows, kv_local, HD)
    scores = jnp.einsum("igrd,jgd->grij", query4, keys3, preferred_element_type=f32) * factor
    masked = jnp.where(allowed[None, None], scores, -1e30)
    top = jnp.max(masked, -1, keepdims=True)
    expo = jnp.exp(masked - top)
    attend = expo / jnp.sum(expo, -1, keepdims=True)
    attend_b = attend.astype(bf16)
    heads4 = jnp.einsum("grij,jgd->igrd", attend_b, values3, preferred_element_type=f32).astype(
        bf16
    )
    heads = heads4.reshape(tok_rows, -1)
    out_part = jnp.dot(heads, w_output, preferred_element_type=f32)
    grad_heads = contract_last(full_grad, w_output).astype(bf16)
    grad4 = grad_heads.reshape(tok_rows, kv_local, group, HD)
    delta = jnp.sum(grad4.astype(f32) * heads4.astype(f32), -1).transpose(1, 2, 0)
    dprob = jnp.einsum("igrd,jgd->grij", grad4, values3, preferred_element_type=f32)
    score_grad = (attend * (dprob - delta[..., None])).astype(bf16)
    query_grad = (
        jnp.einsum("grij,jgd->igrd", score_grad, keys3, preferred_element_type=f32) * factor
    )
    key_part = jnp.einsum("grij,igrd->jgd", score_grad, query4, preferred_element_type=f32) * factor
    value_part = jnp.einsum("grij,igrd->jgd", attend_b, grad4, preferred_element_type=f32)
    key_grad, value_grad = (
        lax.psum_scatter(
            key_part.reshape(all_rows, -1).astype(jnp.bfloat16),
            "seq",
            scatter_dimension=0,
            tiled=True,
        ).astype(jnp.float32),
        lax.psum_scatter(
            value_part.reshape(all_rows, -1).astype(jnp.bfloat16),
            "seq",
            scatter_dimension=0,
            tiled=True,
        ).astype(jnp.float32),
    )
    pre_q = rotate_back(query_grad.reshape(tok_rows, -1), cosine, sine, HD).astype(bf16)
    pre_k = rotate_back(key_grad, cosine, sine, HD).astype(bf16)
    pre_v = value_grad.astype(bf16)
    grad_part = (
        contract_last(pre_q, w_query) + contract_last(pre_k, w_key) + contract_last(pre_v, w_value)
    )
    out_sum, grad_sum = (
        lax.psum_scatter(
            out_part.astype(jnp.bfloat16), "tensor", scatter_dimension=1, tiled=True
        ).astype(jnp.float32),
        lax.psum_scatter(
            grad_part.astype(jnp.bfloat16), "tensor", scatter_dimension=1, tiled=True
        ).astype(jnp.float32),
    )
    layer_out = out_sum.astype(bf16)
    grad_tokens = grad_sum.astype(bf16)
    rows_cat = jnp.concatenate([pre_q, pre_k, pre_v], 1)
    merged = lax.psum_scatter(
        jnp.concatenate(
            [contract_first(full_x, rows_cat), contract_first(full_grad, heads)], 1
        ).astype(jnp.bfloat16),
        "seq",
        scatter_dimension=0,
        tiled=True,
    ).astype(jnp.float32)
    q_width = w_query.shape[1]
    k_width = w_key.shape[1]
    grad_query = merged[:, :q_width]
    grad_key = merged[:, q_width : q_width + k_width]
    grad_value = merged[:, q_width + k_width : q_width + 2 * k_width]
    grad_output = merged[:, q_width + 2 * k_width :].T
    return (layer_out, grad_tokens, grad_query, grad_key, grad_value, grad_output)


def solution(mesh):
    in_specs = (
        P("seq", "tensor"),
        P("seq", "tensor"),
        P(None, "tensor"),
        P(None, "tensor"),
        P(None, "tensor"),
        P("tensor", None),
        P(),
        P(),
    )
    out_specs = (
        P("seq", "tensor"),
        P("seq", "tensor"),
        P("seq", "tensor"),
        P("seq", "tensor"),
        P("seq", "tensor"),
        P("tensor", "seq"),
    )
    return jax.shard_map(
        on_device, mesh=mesh, in_specs=in_specs, out_specs=out_specs, check_vma=False
    )
```

profile of v0, /device:TPU:0, one launch (start us, length us, event | category | flops | bytes accessed | tf_op | source)
XLA Modules:
  0.0 776.4 jit_solution(17244558921709275893)
XLA Ops:
  7.2 0.7 all-gather.5.cloned.1.call-update
  7.9 0.7 all-gather.11.cloned.1.call-update
  9.9 0.8 dynamic_slice.3
  10.7 1.2 fusion.15
  11.9 81.2 %all-gather.5.cloned.1.call-done = bf16[256,8192]{1,0:T(8,128)(2,1)} async-done(((bf16[256,2048]{1,0:T(8,128)(2,1)}), bf16[256,8192]{1,0:T(8,128)(2,1)}) %all-gather.5.cloned.1.call-update) | async-done | bytes 4194320 | tf_op jit(solution)/shard_map/all_gather | solution.py:62
  93.1 11.8 %convolution_bitcast_fusion.2 = f32[32,8,8,128]{3,1,2,0:T(8,128)S(1)} fusion(bf16[256,8192]{1,0:T(8,128)(2,1)} %all-gather.5.cloned.1.call-done, bf16[8192,1024]{1,0:T(8,128)(2,1)} %param.10), kind=kOutput, calls=%fused_computation.29 | convolution fusion | flops 4294967296 | bytes 22020096 | tf_op jit(solution)/shard_map/dot_general | solution.py:65
  106.0 1.1 copy-done.1
  107.0 1.8 fusion.32
  108.9 0.7 pad_maximum_fusion.3
  109.7 64.3 %all-gather.11.cloned.1.call-done = bf16[256,8192]{1,0:T(8,128)(2,1)} async-done(((bf16[256,2048]{1,0:T(8,128)(2,1)}), bf16[256,8192]{1,0:T(8,128)(2,1)}) %all-gather.11.cloned.1.call-update) | async-done | bytes 4194320 | tf_op jit(solution)/shard_map/all_gather | solution.py:63
  174.0 11.6 %convolution_convert_fusion.3 = bf16[256,1024]{1,0:T(8,128)(2,1)S(1)} fusion(bf16[256,8192]{1,0:T(8,128)(2,1)} %all-gather.11.cloned.1.call-done, bf16[1024,8192]{1,0:T(8,128)(2,1)} %param.13), kind=kOutput, calls=%fused_computation.32 | convolution fusion | flops 4295229440 | bytes 21495808 | tf_op jit(solution)/shard_map/dot_general | solution.py:41
  185.7 5.4 convolution_convert_fusion.4
  191.4 7.2 all-gather.9.cloned.1.call-done
  198.6 12.5 %fusion.31 = (f32[2,4,256]{2,1,0:T(4,128)S(1)}, f32[2,4,256,2048]{2,3,1,0:T(8,128)}) fusion(pred[256,2048]{0,1:T(8,128)(4,1)S(1)} %fusion.15, bf16[2048,2,128,1]{0,2,3,1:T(8,128)(2,1)} %bitcast.126, bf16[256,2,4,128]{3,0,2,1:T(8,128)(2,1)S(1)} %bitcast.122), kind=kOutput, calls=%fused_computation.67 | convolution fusion | flops 1090521088 | bytes 18882560 | tf_op jit(solution)/shard_map/sub | solution.py:89
  211.0 9.3 %fusion.9 = bf16[2,4,256,2048]{2,3,1,0:T(8,128)(2,1)} fusion(f32[2,4,256,2048]{2,3,1,0:T(8,128)} %get-tuple-element.33, f32[2,4,256]{2,1,0:T(4,128)S(1)} %get-tuple-element.32), kind=kLoop, calls=%fused_computation.19 | loop fusion | flops 8388608 | bytes 25174016 | tf_op jit(solution)/shard_map/convert_element_type | solution.py:91
  220.4 4.0 all-gather.7.cloned.1.call-done
  224.4 1.3 reshape.161
  225.7 4.8 multiply_reduce_fusion
  230.5 7.1 fusion.3
  237.6 3.2 copy-done
  240.8 3.9 fusion.13
  245.0 4.7 convolution_multiply_fusion
  249.7 0.9 fusion.30
  250.6 1.5 copy.74
  252.1 1.3 copy.75
  253.4 1.6 add_convert_fusion
  255.4 7.3 fusion.14
  262.8 10.5 %convert_bitcast_fusion = bf16[8192,1024]{0,1:T(8,128)(2,1)} fusion(bf16[256,1024]{0,1:T(8,128)(2,1)S(1)} %bitcast.110, bf16[256,8192]{1,0:T(8,128)(2,1)} %all-gather.11.cloned.1.call-done), kind=kOutput, calls=%fused_computation.8 | convolution fusion | flops 4303355904 | bytes 21495808 | tf_op jit(solution)/shard_map/dot_general | solution.py:47
  273.2 7.7 reduce-scatter.8.cloned.1.call-done
  281.0 0.9 convert.43
  282.0 38.5 %reduce-scatter.10.cloned.1.call-done = bf16[256,256]{0,1:T(8,128)(2,1)} async-done(((bf16[2048,256]{0,1:T(8,128)(2,1)}), bf16[256,256]{0,1:T(8,128)(2,1)}) %reduce-scatter.10.cloned.1.call-update) | async-done | bytes 131088 | tf_op jit(solution)/shard_map/reduce_scatter | solution.py:114
  320.6 1.0 copy.50
  321.6 14.0 %fusion.1 = bf16[8192,1536]{0,1:T(8,128)(2,1)} fusion(bf16[256,8192]{1,0:T(8,128)(2,1)} %all-gather.5.cloned.1.call-done, bf16[256,256]{1,0:T(8,128)(2,1)S(1)} %copy.50, bf16[256,256]{1,0:T(8,128)(2,1)S(1)} %copy.49, bf16[256,1024]{1,0:T(8,128)(2,1)S(1)} %bitcast.121), kind=kOutput, calls=%fused_computation.3 | convolution fusion | flops 6457393152 | bytes 30146560 | tf_op jit(solution)/shard_map/dot_general | solution.py:47
  335.6 29.0 %pad_maximum_fusion = bf16[8192,2560]{0,1:T(8,128)(2,1)} fusion(bf16[8192,1024]{0,1:T(8,128)(2,1)} %convert_bitcast_fusion, bf16[8192,1536]{0,1:T(8,128)(2,1)} %fusion.1), kind=kLoop, calls=%fused_computation.1 | loop fusion | flops 83886080 | bytes 83886080 | tf_op jit(solution)/shard_map/concatenate | solution.py:139
  364.9 12.7 %convolution_convert_fusion.1 = bf16[256,8192]{1,0:T(8,128)(2,1)} fusion(bf16[256,1024]{0,1:T(8,128)(2,1)S(1)} %bitcast.111, bf16[1024,8192]{1,0:T(8,128)(2,1)} %param.13), kind=kOutput, calls=%fused_computation.13 | convolution fusion | flops 4297064448 | bytes 21495808 | tf_op jit(solution)/shard_map/dot_general | solution.py:96
  377.7 23.1 %fusion.28 = f32[256,8192]{1,0:T(8,128)} fusion(bf16[8192,1024]{1,0:T(8,128)(2,1)} %param.10, bf16[32,8,8,128]{3,2,1,0:T(8,128)(2,1)S(1)} %bitcast.115), kind=kOutput, calls=%fused_computation.64 | convolution fusion | flops 4294967296 | bytes 25690112 | tf_op jit(solution)/shard_map/dot_general | solution.py:41
  400.8 8.9 %convolution_add_fusion.1 = f32[256,8192]{1,0:T(8,128)S(1)} fusion(f32[256,8192]{1,0:T(8,128)} %fusion.28, bf16[256,256]{0,1:T(8,128)(2,1)S(1)} %bitcast.125, bf16[8192,256]{1,0:T(8,128)(2,1)} %param.11), kind=kOutput, calls=%fused_computation.12 | convolution fusion | flops 1075838976 | bytes 21102592 | tf_op jit(solution)/shard_map/dot_general | solution.py:41
  410.3 3.7 fusion.5
  414.1 195.4 %reduce-scatter.14.cloned.1.call-done = bf16[1024,2560]{0,1:T(8,128)(2,1)} async-done(((bf16[8192,2560]{0,1:T(8,128)(2,1)}), bf16[1024,2560]{0,1:T(8,128)(2,1)}) %reduce-scatter.14.cloned.1.call-update) | async-done | bytes 5242896 | tf_op jit(solution)/shard_map/reduce_scatter | solution.py:138
  609.5 4.1 slice.56
  613.6 5.3 copy.51
  618.9 1.5 fusion.29
  620.5 1.3 copy.52
  621.8 1.3 copy.53
  623.1 3.8 convert_element_type.104
  626.9 2.3 slice_bitcast_fusion
  629.2 60.1 %reduce-scatter.6.cloned.1.call-done = bf16[256,2048]{1,0:T(8,128)(2,1)} async-done(((bf16[256,8192]{1,0:T(8,128)(2,1)}), bf16[256,2048]{1,0:T(8,128)(2,1)}) %reduce-scatter.6.cloned.1.call-update) | async-done | bytes 1048592 | tf_op jit(solution)/shard_map/reduce_scatter | solution.py:128
  689.3 80.2 %reduce-scatter.12.cloned.1.call-done = bf16[256,2048]{1,0:T(8,128)(2,1)} async-done(((bf16[256,8192]{1,0:T(8,128)(2,1)}), bf16[256,2048]{1,0:T(8,128)(2,1)}) %reduce-scatter.12.cloned.1.call-update) | async-done | bytes 1048592 | tf_op jit(solution)/shard_map/reduce_scatter | solution.py:131
  (43 shorter events, 4.1 us)
Async XLA Ops:
  7.2 85.9 %all-gather.5.cloned.1.call-start = ((), (), s32[]{:S(2)}) async-start(), calls=%async_computation.5 | async-start | bytes 5242880 | tf_op jit(solution)/shard_map/all_gather | solution.py:62
  7.9 166.1 %all-gather.11.cloned.1.call-start = ((), (), s32[]{:S(2)}) async-start(), calls=%async_computation.9 | async-start | bytes 5242880 | tf_op jit(solution)/shard_map/all_gather | solution.py:63
  8.6 189.9 %all-gather.9.cloned.1.call-start = ((), (), s32[]{:S(2)}) async-start(), calls=%async_computation.7 | async-start | bytes 1179648 | tf_op jit(solution)/shard_map/all_gather | solution.py:75
  93.1 12.9 %copy-start.2 = (bf16[256,8192]{1,0:T(8,128)(2,1)S(1)}, bf16[256,8192]{1,0:T(8,128)(2,1)}, u32[]{:S(2)}) copy-start(bf16[256,8192]{1,0:T(8,128)(2,1)} %all-gather.5.cloned.1.call-done) | copy-start | bytes 12582916
  104.9 2.2 copy-start.1
  109.6 114.8 %all-gather.7.cloned.1.call-start = ((), (), s32[]{:S(2)}) async-start(), calls=%async_computation.6 | async-start | bytes 1179648 | tf_op jit(solution)/shard_map/all_gather | solution.py:76
  191.1 89.8 %reduce-scatter.8.cloned.1.call-start = ((), (), s32[]{:S(2)}) async-start(), calls=%async_computation.10 | async-start | bytes 1179648 | tf_op jit(solution)/shard_map/reduce_scatter | solution.py:108
  237.6 3.2 copy-start
  240.8 4.2 copy-start.4
  244.8 75.8 %reduce-scatter.10.cloned.1.call-start = ((), (), s32[]{:S(2)}) async-start(), calls=%async_computation.11 | async-start | bytes 1179648 | tf_op jit(solution)/shard_map/reduce_scatter | solution.py:114
  262.7 346.8 %reduce-scatter.14.cloned.1.call-start = ((), (), s32[]{:S(2)}) async-start(), calls=%async_computation.13 | async-start | bytes 47185920 | tf_op jit(solution)/shard_map/reduce_scatter | solution.py:138
  364.6 324.7 %reduce-scatter.6.cloned.1.call-start = ((), (), s32[]{:S(2)}) async-start(), calls=%async_computation.8 | async-start | bytes 5242880 | tf_op jit(solution)/shard_map/reduce_scatter | solution.py:128
  377.6 391.8 %reduce-scatter.12.cloned.1.call-start = ((), (), s32[]{:S(2)}) async-start(), calls=%async_computation.12 | async-start | bytes 5242880 | tf_op jit(solution)/shard_map/reduce_scatter | solution.py:131
  400.8 9.5 %copy-start.3 = (bf16[8192,256]{1,0:T(8,128)(2,1)S(1)}, bf16[8192,256]{1,0:T(8,128)(2,1)}, u32[]{:S(2)}) copy-start(bf16[8192,256]{1,0:T(8,128)(2,1)} %param.12) | copy-start | bytes 12582916
  400.8 9.5 %copy-start.5 = (bf16[256,256]{0,1:T(8,128)(2,1)S(1)}, bf16[256,256]{0,1:T(8,128)(2,1)}, u32[]{:S(2)}) copy-start(bf16[256,256]{0,1:T(8,128)(2,1)} %reduce-scatter.10.cloned.1.call-done) | copy-start | bytes 393220
Sparse Core Ops, SparseCore 0:
  9.6 83.4 all-gather.4
  94.6 79.2 all-gather.10
  176.4 22.0 all-gather.8
  200.9 23.4 all-gather.6
  244.9 36.0 reduce-scatter.7
  284.6 35.9 reduce-scatter.9
  364.7 244.7 reduce-scatter.13
  612.5 76.7 reduce-scatter.5
  692.2 77.2 reduce-scatter.11
where the time goes:
time: 785 us; the launch traced here: 776 us
  waiting for transfers between devices  540 us (69%)
  matrix products  144 us (18%)
  other arithmetic  48.1 us (6%)
  local copies, waits for them, and re-layouts  28.4 us (4%)
  between operations  15.2 us (2%)
    reduce_scatter x1, waiting for transfers between devices, on_device(): lax.psum_scatter(jnp.concatenate([contract_first(full_x, rows_cat), contr...  195 us
    all_gather x1, waiting for transfers between devices, on_device(): lax.all_gather(tokens, 'tensor', axis=1, tiled=True)  81.2 us
    reduce_scatter x1, waiting for transfers between devices, on_device(): lax.psum_scatter(grad_part.astype(jnp.bfloat16), 'tensor', scatter_dimens...  80.2 us
    all_gather x1, waiting for transfers between devices, on_device(): lax.all_gather(cotangent, 'tensor', axis=1, tiled=True)  64.3 us
    reduce_scatter x1, waiting for transfers between devices, on_device(): lax.psum_scatter(out_part.astype(jnp.bfloat16), 'tensor', scatter_dimensi...  60.1 us
    dot_general x4, matrix products, contract_last(): lax.dot_general(left, right, (((1,), (1,)), ((), ())), preferred_element_...  47.3 us
    reduce_scatter x1, waiting for transfers between devices, on_device(): lax.psum_scatter(value_part.reshape(all_rows, -1).astype(jnp.bfloat16), '...  38.5 us
    concatenate x1, other arithmetic, on_device(): jnp.concatenate([contract_first(full_x, rows_cat), contract_first(full_gr...  29 us
  transfers between devices with their start and end apart: 9, of which 9 were waited for; matrix products, arithmetic and copies ran while one was open for 20% of the time, Pallas kernels for 0%

commit v1 on v0

--- a/solution.py
+++ b/solution.py
@@ -49,6 +49,50 @@
     )
 
 
+def swap(value, step):
+    count = lax.axis_size("seq")
+    return lax.ppermute(value, "seq", [(i, i ^ step) for i in range(count)])
+
+
+def block_order(count):
+    return list(range(0, count, 2)) + list(range(1, count, 2))
+
+
+def gather_blocks(value):
+    count = lax.axis_size("seq")
+    even = [value] + [swap(value, step) for step in range(2, count, 2)]
+    odd = [swap(piece, 1) for piece in even]
+    return even + odd
+
+
+def scatter_sum(pieces):
+    f32 = jnp.float32
+    half = len(pieces) // 2
+    given = [swap(piece.astype(jnp.bfloat16), 1) for piece in pieces[half:]]
+    paired = [pieces[k].astype(f32) + given[k].astype(f32) for k in range(half)]
+    total = paired[0]
+    for k in range(1, half):
+        total = total + swap(paired[k].astype(jnp.bfloat16), 2 * k).astype(f32)
+    return total
+
+
+def reshard_columns(full):
+    return lax.all_to_all(full, "seq", 1, 0, tiled=True)
+
+
+def in_order(pieces, me):
+    count = len(pieces)
+    rows, columns = pieces[0].shape
+    whole = jnp.zeros((count * rows, columns), pieces[0].dtype)
+    for piece, step in zip(pieces, block_order(count)):
+        whole = lax.dynamic_update_slice(whole, piece, ((me ^ step) * rows, 0))
+    return whole
+
+
+def after(value, *earlier):
+    return lax.optimization_barrier((value, *earlier))[0]
+
+
 def on_device(tokens, cotangent, w_query, w_key, w_value, w_output, segments, band):
     f32 = jnp.float32
     bf16 = jnp.bfloat16
@@ -56,28 +100,37 @@
     tok_rows = tokens.shape[0]
     seq_count = lax.axis_size("seq")
     all_rows = tok_rows * seq_count
-    kv_local = w_key.shape[1] // HD
-    group = w_query.shape[1] // w_key.shape[1]
-    full_x, full_grad = (
-        lax.all_gather(tokens, "tensor", axis=1, tiled=True),
-        lax.all_gather(cotangent, "tensor", axis=1, tiled=True),
-    )
-    proj_q = jnp.dot(full_x, w_query, preferred_element_type=f32)
+    q_width = w_query.shape[1]
+    k_width = w_key.shape[1]
+    kv_local = k_width // HD
+    group = q_width // k_width
+    me = lax.axis_index("seq")
+    order = block_order(seq_count)
+
+    full_x = lax.all_gather(tokens, "tensor", axis=1, tiled=True)
+    full_grad = lax.all_gather(after(cotangent, full_x), "tensor", axis=1, tiled=True)
+
+    first_row = me * tok_rows
+    own_rows = first_row + jnp.arange(tok_rows)
+    cosine, sine = tables(own_rows.astype(f32), HD)
     proj_k = jnp.dot(full_x, w_key, preferred_element_type=f32)
     proj_v = jnp.dot(full_x, w_value, preferred_element_type=f32)
-    first_row = lax.axis_index("seq") * tok_rows
-    own_rows = first_row + jnp.arange(tok_rows)
-    cosine, sine = tables(own_rows.astype(f32), HD)
-    query = rotate(proj_q, cosine, sine, HD).astype(bf16)
     keys_local = rotate(proj_k, cosine, sine, HD).astype(bf16)
     values_local = proj_v.astype(bf16)
-    keys, values = (
-        lax.all_gather(keys_local, "seq", axis=0, tiled=True),
-        lax.all_gather(values_local, "seq", axis=0, tiled=True),
-    )
-    key_rows = jnp.arange(all_rows)
+    kv_pieces = gather_blocks(jnp.concatenate([keys_local, values_local], 1))
+    kv_all = jnp.concatenate(kv_pieces, 0)
+    keys, values = kv_all[:, :k_width], kv_all[:, k_width:]
+    proj_q = jnp.dot(full_x, w_query, preferred_element_type=f32)
+    query = rotate(proj_q, cosine, sine, HD).astype(bf16)
+
+    x_cols = reshard_columns(full_x)
+
+    key_rows = jnp.concatenate([(me ^ step) * tok_rows + jnp.arange(tok_rows) for step in order])
+    key_seg = jnp.concatenate(
+        [lax.dynamic_slice_in_dim(segments, (me ^ step) * tok_rows, tok_rows) for step in order]
+    )
     own_seg = lax.dynamic_slice_in_dim(segments, first_row, tok_rows)
-    allowed = (own_seg[:, None] == segments[None, :]) & (
+    allowed = (own_seg[:, None] == key_seg[None, :]) & (
         key_rows[None, :] <= own_rows[:, None] + band[0]
     )
     query4 = query.reshape(tok_rows, kv_local, group, HD)
@@ -93,8 +146,13 @@
         bf16
     )
     heads = heads4.reshape(tok_rows, -1)
-    out_part = jnp.dot(heads, w_output, preferred_element_type=f32)
-    grad_heads = contract_last(full_grad, w_output).astype(bf16)
+    out_part = jnp.dot(heads, w_output, preferred_element_type=f32).astype(bf16)
+    layer_out = lax.psum_scatter(out_part, "tensor", scatter_dimension=1, tiled=True)
+
+    full_grad = after(full_grad, out_part)
+    g_cols = reshard_columns(full_grad)
+    heads_all = in_order(gather_blocks(heads), me)
+    grad_heads = after(contract_last(full_grad, w_output).astype(bf16), x_cols)
     grad4 = grad_heads.reshape(tok_rows, kv_local, group, HD)
     delta = jnp.sum(grad4.astype(f32) * heads4.astype(f32), -1).transpose(1, 2, 0)
     dprob = jnp.einsum("igrd,jgd->grij", grad4, values3, preferred_element_type=f32)
@@ -104,51 +162,26 @@
     )
     key_part = jnp.einsum("grij,igrd->jgd", score_grad, query4, preferred_element_type=f32) * factor
     value_part = jnp.einsum("grij,igrd->jgd", attend_b, grad4, preferred_element_type=f32)
-    key_grad, value_grad = (
-        lax.psum_scatter(
-            key_part.reshape(all_rows, -1).astype(jnp.bfloat16),
-            "seq",
-            scatter_dimension=0,
-            tiled=True,
-        ).astype(jnp.float32),
-        lax.psum_scatter(
-            value_part.reshape(all_rows, -1).astype(jnp.bfloat16),
-            "seq",
-            scatter_dimension=0,
-            tiled=True,
-        ).astype(jnp.float32),
-    )
+    kv_part = jnp.concatenate(
+        [key_part.reshape(all_rows, -1), value_part.reshape(all_rows, -1)], 1
+    ).astype(bf16)
+    kv_part = after(kv_part, g_cols)
+    kv_grad = scatter_sum([kv_part[k * tok_rows : (k + 1) * tok_rows] for k in range(seq_count)])
     pre_q = rotate_back(query_grad.reshape(tok_rows, -1), cosine, sine, HD).astype(bf16)
-    pre_k = rotate_back(key_grad, cosine, sine, HD).astype(bf16)
-    pre_v = value_grad.astype(bf16)
+    pre_k = rotate_back(kv_grad[:, :k_width], cosine, sine, HD).astype(bf16)
+    pre_v = kv_grad[:, k_width:].astype(bf16)
     grad_part = (
         contract_last(pre_q, w_query) + contract_last(pre_k, w_key) + contract_last(pre_v, w_value)
-    )
-    out_sum, grad_sum = (
-        lax.psum_scatter(
-            out_part.astype(jnp.bfloat16), "tensor", scatter_dimension=1, tiled=True
-        ).astype(jnp.float32),
-        lax.psum_scatter(
-            grad_part.astype(jnp.bfloat16), "tensor", scatter_dimension=1, tiled=True
-        ).astype(jnp.float32),
-    )
-    layer_out = out_sum.astype(bf16)
-    grad_tokens = grad_sum.astype(bf16)
-    rows_cat = jnp.concatenate([pre_q, pre_k, pre_v], 1)
-    merged = lax.psum_scatter(
-        jnp.concatenate(
-            [contract_first(full_x, rows_cat), contract_first(full_grad, heads)], 1
-        ).astype(jnp.bfloat16),
-        "seq",
-        scatter_dimension=0,
-        tiled=True,
-    ).astype(jnp.float32)
-    q_width = w_query.shape[1]
-    k_width = w_key.shape[1]
+    ).astype(bf16)
+    grad_tokens = lax.psum_scatter(grad_part, "tensor", scatter_dimension=1, tiled=True)
+
+    pre_cat = after(jnp.concatenate([pre_q, pre_k, pre_v], 1), heads_all)
+    pre_all = in_order(gather_blocks(pre_cat), me)
+    grad_output = contract_first(heads_all, g_cols)
+    merged = contract_first(x_cols, pre_all)
     grad_query = merged[:, :q_width]
     grad_key = merged[:, q_width : q_width + k_width]
-    grad_value = merged[:, q_width + k_width : q_width + 2 * k_width]
-    grad_output = merged[:, q_width + 2 * k_width :].T
+    grad_value = merged[:, q_width + k_width :]
     return (layer_out, grad_tokens, grad_query, grad_key, grad_value, grad_output)
 
 

time: 785 us -> 416 us (0.53)
  waiting for transfers between devices: 540 us -> 175 us
  local copies, waits for them, and re-layouts: 28.4 us -> 62.7 us
  other arithmetic: 48.1 us -> 15.7 us
  matrix products: 144 us -> 112 us
  starting transfers between devices: 1 us -> 26.8 us
    reduce_scatter x5 -> x2, waiting for transfers between devices: 382 us -> 0.01 us  [the longest x1 0.01 us: on_device(): lax.psum_scatter(out_part, 'tensor', scatter_dimension=1, tiled=True)]
    all_gather x4 -> x2, waiting for transfers between devices: 157 us -> 93.8 us  [the longest x1 75.2 us: on_device(): full_x = lax.all_gather(tokens, 'tensor', axis=1, tiled=True)]
    ppermute x0 -> x28, waiting for transfers between devices: none -> 48.2 us  [swap(): return lax.ppermute(value, 'seq', [(i, i ^ step) for i in range(count)])]
    all_to_all x0 -> x2, waiting for transfers between devices: none -> 32.8 us  [reshard_columns(): return lax.all_to_all(full, 'seq', 1, 0, tiled=True)]
    concatenate x1 -> x4, other arithmetic: 29 us -> 1.12 us  [the longest x1 0.82 us: on_device(): kv_pieces = gather_blocks(jnp.concatenate([keys_local, values_local], 1))]
    unnamed x19 -> x57, local copies, waits for them, and re-layouts: 16 us -> 36.6 us
    ppermute x0 -> x28, starting transfers between devices: none -> 17.4 us  [swap(): return lax.ppermute(value, 'seq', [(i, i ^ step) for i in range(count)])]
    all_to_all x0 -> x2, local copies, waits for them, and re-layouts: none -> 12.9 us  [reshard_columns(): return lax.all_to_all(full, 'seq', 1, 0, tiled=True)]
  transfers between devices with their start and end apart: 9 -> 34, of which waited for: 9 -> 12; matrix products, arithmetic and copies ran while one was open for 20% -> 41% of each run, Pallas kernels for 0% -> 0%
where the time goes in v1:
time: 416 us; the launch traced here: 408 us
  waiting for transfers between devices  175 us (42%)
  matrix products  112 us (27%)
  local copies, waits for them, and re-layouts  62.7 us (15%)
  starting transfers between devices  26.8 us (6%)
  other arithmetic  15.7 us (4%)
  between operations  15.5 us (4%)
    all_gather x1, waiting for transfers between devices, on_device(): full_x = lax.all_gather(tokens, 'tensor', axis=1, tiled=True)  75.2 us
    ppermute x28, waiting for transfers between devices, swap(): return lax.ppermute(value, 'seq', [(i, i ^ step) for i in range(count)])  48.2 us
    dot_general x4, matrix products, contract_last(): lax.dot_general(left, right, (((1,), (1,)), ((), ())), preferred_element_...  40.1 us
    unnamed x57, local copies, waits for them, and re-layouts  36.6 us
    all_to_all x2, waiting for transfers between devices, reshard_columns(): return lax.all_to_all(full, 'seq', 1, 0, tiled=True)  32.8 us
    all_gather x1, waiting for transfers between devices, on_device(): lax.all_gather(after(cotangent, full_x), 'tensor', axis=1, tiled=True)  18.7 us
    ppermute x28, starting transfers between devices, swap(): return lax.ppermute(value, 'seq', [(i, i ^ step) for i in range(count)])  17.4 us
    dot_general x2, matrix products, contract_first(): lax.dot_general(left, right, (((0,), (0,)), ((), ())), preferred_element_...  17 us
  transfers between devices with their start and end apart: 34, of which 12 were waited for; matrix products, arithmetic and copies ran while one was open for 41% of the time, Pallas kernels for 0%

profile of v1, /device:TPU:0, one launch (start us, length us, event | category | flops | bytes accessed | tf_op | source)
XLA Modules:
  0.0 408.1 jit_solution(2995070585059447947)
XLA Ops:
  7.2 2.3 copy.52
  18.5 75.2 %all-gather.3.cloned.1.call-done = bf16[256,8192]{0,1:T(8,128)(2,1)} async-done(((bf16[256,2048]{0,1:T(8,128)(2,1)}), bf16[256,8192]{0,1:T(8,128)(2,1)}) %all-gather.3.cloned.1.call-update) | async-done | bytes 4194320 | tf_op jit(solution)/shard_map/all_gather | solution.py:110
  93.6 5.3 %fusion.25 = f32[256,256]{0,1:T(8,128)S(1)} fusion(bf16[256,8192]{0,1:T(8,128)(2,1)} %all-gather.3.cloned.1.call-done, bf16[8192,256]{1,0:T(8,128)(2,1)} %param.11), kind=kOutput, calls=%fused_computation.106 | convolution fusion | flops 1073741824 | bytes 8650752 | tf_op jit(solution)/shard_map/dot_general | solution.py:116
  99.0 5.9 %convolution_convert_fusion.3 = bf16[256,256]{0,1:T(8,128)(2,1)S(1)} fusion(bf16[256,8192]{0,1:T(8,128)(2,1)} %all-gather.3.cloned.1.call-done, bf16[8192,256]{1,0:T(8,128)(2,1)} %param.12), kind=kOutput, calls=%fused_computation.29 | convolution fusion | flops 1073807360 | bytes 8519680 | tf_op jit(solution)/shard_map/dot_general | solution.py:117
  105.8 1.5 collective-permute-start
  107.3 1.5 collective-permute-start.1
  109.3 6.5 %convolution_bitcast_fusion.3 = f32[32,8,8,128]{3,1,2,0:T(8,128)S(1)} fusion(bf16[256,8192]{0,1:T(8,128)(2,1)} %all-gather.3.cloned.1.call-done, bf16[8192,1024]{1,0:T(8,128)(2,1)S(1)} %copy-done), kind=kOutput, calls=%fused_computation.25 | convolution fusion | flops 4294967296 | bytes 22020096 | tf_op jit(solution)/shard_map/dot_general | solution.py:123
  118.2 4.5 %all-to-all-start = ((bf16[256,8,1024]{0,2,1:T(8,128)(2,1)}), bf16[256,8,1024]{0,2,1:T(8,128)(2,1)}, u32[]{:S(2)}, u32[]{:S(2)}) async-start(bf16[256,8,1024]{0,2,1:T(8,128)(2,1)} %bitcast.118), calls=%async_computation.1 | async-start | bytes 8388608 | tf_op jit(solution)/shard_map/all_to_all | solution.py:80
  123.5 1.7 constant_dynamic-update-slice_fusion.6
  125.3 1.7 constant_dynamic-update-slice_fusion.5
  127.4 1.7 constant_dynamic-update-slice_fusion.4
  129.1 1.7 constant_dynamic-update-slice_fusion.3
  132.9 1.7 fusion.21
  134.7 9.4 %fusion.23 = (f32[2,4,256]{2,1,0:T(4,128)S(1)}, f32[2,4,256,2048]{2,3,1,0:T(8,128)}) fusion(pred[256,2048]{0,1:T(8,128)(4,1)S(1)} %compare_and_fusion, bf16[2048,2,128,1]{0,2,3,1:T(8,128)(2,1)S(1)} %bitcast.136, bf16[256,2,4,128]{3,0,2,1:T(8,128)(2,1)S(1)} %bitcast.142), kind=kOutput, calls=%fused_computation.104 | convolution fusion | flops 1090521088 | bytes 18882560 | tf_op jit(solution)/shard_map/sub | solution.py:142
  144.1 7.4 %fusion.8 = bf16[2,4,256,2048]{2,3,1,0:T(8,128)(2,1)S(1)} fusion(f32[2,4,256,2048]{2,3,1,0:T(8,128)} %get-tuple-element.62, f32[2,4,256]{2,1,0:T(4,128)S(1)} %get-tuple-element.61), kind=kLoop, calls=%fused_computation.15 | loop fusion | flops 8388608 | bytes 25174016 | tf_op jit(solution)/shard_map/convert_element_type | solution.py:144
  152.8 3.0 copy-done.1
  156.6 1.5 slice-done.3
  158.1 6.4 %convolution_convert_fusion = bf16[256,8192]{1,0:T(8,128)(2,1)} fusion(bf16[256,1024]{0,1:T(8,128)(2,1)S(1)} %bitcast.122, bf16[1024,8192]{1,0:T(8,128)(2,1)S(1)} %bitcast.120), kind=kOutput, calls=%fused_computation.9 | convolution fusion | flops 4297064448 | bytes 21495808 | tf_op jit(solution)/shard_map/dot_general | solution.py:149
  164.6 7.3 %all-to-all-done = bf16[256,8,1024]{0,2,1:T(8,128)(2,1)} async-done(((bf16[256,8,1024]{0,2,1:T(8,128)(2,1)}), bf16[256,8,1024]{0,2,1:T(8,128)(2,1)}, u32[]{:S(2)}, u32[]{:S(2)}) %all-to-all-start) | async-done | bytes 4194336 | tf_op jit(solution)/shard_map/all_to_all | solution.py:80
  171.9 6.4 %copy.59 = bf16[8,256,1024]{2,1,0:T(8,128)(2,1)} copy(bf16[8,256,1024]{1,2,0:T(8,128)(2,1)} %bitcast.16) | data formatting | bytes 8388608 | tf_op jit(solution)/shard_map/all_to_all | solution.py:80
  178.3 18.7 %all-gather.5.cloned.1.call-done = bf16[256,8192]{0,1:T(8,128)(2,1)} async-done(((bf16[256,2048]{0,1:T(8,128)(2,1)}), bf16[256,8192]{0,1:T(8,128)(2,1)}) %all-gather.5.cloned.1.call-update) | async-done | bytes 4194320 | tf_op jit(solution)/shard_map/all_gather | solution.py:111
  196.9 11.6 %convolution_convert_fusion.2 = bf16[256,1024]{1,0:T(8,128)(2,1)S(1)} fusion(bf16[256,8192]{0,1:T(8,128)(2,1)} %all-gather.5.cloned.1.call-done, bf16[1024,8192]{1,0:T(8,128)(2,1)} %param.13), kind=kOutput, calls=%fused_computation.28 | convolution fusion | flops 4295229440 | bytes 21495808 | tf_op jit(solution)/shard_map/dot_general | solution.py:41
  208.9 4.6 %all-to-all-start.1 = ((bf16[256,8,1024]{0,2,1:T(8,128)(2,1)}), bf16[256,8,1024]{0,2,1:T(8,128)(2,1)}, u32[]{:S(2)}, u32[]{:S(2)}) async-start(bf16[256,8,1024]{0,2,1:T(8,128)(2,1)} %bitcast.135), calls=%async_computation.2 | async-start | bytes 8388608 | tf_op jit(solution)/shard_map/all_to_all | solution.py:80
  213.5 8.0 %fusion.2 = bf16[2,4,256,2048]{2,3,1,0:T(8,128)(2,1)S(1)} fusion(f32[2,4,256]{2,1,0:T(4,128)S(1)} %bitcast.150, f32[2,4,256,2048]{2,3,1,0:T(8,128)} %get-tuple-element.62, f32[2,4,256]{2,1,0:T(4,128)S(1)} %get-tuple-element.61, bf16[2048,2,128,1]{0,2,3,1:T(8,128)(2,1)} %bitcast.139, bf16[256,2,4,128]{0,3,2,1:T(8,128)(2,1)S(1)} %bitcast.130), kind=kOutput, calls=%fused_computation.3 | convolution fusion | flops 1090519040 | bytes 26755072 | tf_op jit(solution)/shard_map/igrd,jgd->grij/dot_general | solution.py:158
  221.5 3.3 convolution_multiply_fusion
  227.6 6.3 %fusion.13 = bf16[2,128,2048]{2,1,0:T(8,128)(2,1)S(1)} fusion(bf16[256,2,4,128]{0,3,2,1:T(8,128)(2,1)S(1)} %bitcast.131, bf16[2,4,256,2048]{2,3,1,0:T(8,128)(2,1)} %copy-done.1), kind=kOutput, calls=%fused_computation.22 | convolution fusion | flops 1074266112 | bytes 9961472 | tf_op jit(solution)/shard_map/grij,igrd->jgd/dot_general | solution.py:164
  233.9 2.9 fusion.12
  237.1 25.6 %all-to-all-done.1 = bf16[256,8,1024]{0,2,1:T(8,128)(2,1)} async-done(((bf16[256,8,1024]{0,2,1:T(8,128)(2,1)}), bf16[256,8,1024]{0,2,1:T(8,128)(2,1)}, u32[]{:S(2)}, u32[]{:S(2)}) %all-to-all-start.1) | async-done | bytes 4194336 | tf_op jit(solution)/shard_map/all_to_all | solution.py:80
  262.6 6.4 %copy.69 = bf16[8,256,1024]{2,1,0:T(8,128)(2,1)} copy(bf16[8,256,1024]{1,2,0:T(8,128)(2,1)} %bitcast.35) | data formatting | bytes 8388608 | tf_op jit(solution)/shard_map/all_to_all | solution.py:80
  270.3 1.8 add_convert_fusion
  276.0 1.5 collective-permute-start.9
  277.5 19.2 %fusion.18 = f32[256,8192]{1,0:T(8,128)} fusion(bf16[8192,1024]{1,0:T(8,128)(2,1)} %param.10, bf16[32,8,8,128]{3,2,1,0:T(8,128)(2,1)S(1)} %bitcast.128), kind=kOutput, calls=%fused_computation.99 | convolution fusion | flops 4294967296 | bytes 25690112 | tf_op jit(solution)/shard_map/dot_general | solution.py:41
  298.2 6.1 %convolution_add_fusion.1 = f32[256,8192]{1,0:T(8,128)S(1)} fusion(f32[256,8192]{1,0:T(8,128)} %fusion.18, bf16[256,256]{0,1:T(8,128)(2,1)S(1)} %bitcast.145, bf16[8192,256]{1,0:T(8,128)(2,1)} %param.11), kind=kOutput, calls=%fused_computation.8 | convolution fusion | flops 1075838976 | bytes 21102592 | tf_op jit(solution)/shard_map/dot_general | solution.py:41
  304.3 3.3 fusion.4
  308.8 2.3 collective-permute-start.16
  311.1 11.4 %collective-permute-done.14 = bf16[256,1024]{0,1:T(8,128)(2,1)S(1)} collective-permute-done((bf16[256,1024]{0,1:T(8,128)(2,1)S(1)}, bf16[256,1024]{0,1:T(8,128)(2,1)S(1)}, u32[]{:S(2)}, u32[]{:S(2)}) %collective-permute-start.14) | collective-permute-done | bytes 524320 | tf_op jit(solution)/shard_map/ppermute | solution.py:54
  323.1 9.1 %collective-permute-done.15 = bf16[256,1024]{0,1:T(8,128)(2,1)S(1)} collective-permute-done((bf16[256,1024]{0,1:T(8,128)(2,1)S(1)}, bf16[256,1024]{0,1:T(8,128)(2,1)S(1)}, u32[]{:S(2)}, u32[]{:S(2)}) %collective-permute-start.15) | collective-permute-done | bytes 524320 | tf_op jit(solution)/shard_map/ppermute | solution.py:54
  335.0 1.9 copy-done.6
  338.1 1.5 collective-permute-start.21
  340.2 1.5 collective-permute-start.23
  341.7 10.0 %fusion.26 = f32[1024,1024]{1,0:T(8,128)} fusion(bf16[2048,1024]{0,1:T(8,128)(2,1)} %copy-done.6, bf16[2048,1024]{1,0:T(8,128)(2,1)} %bitcast.134), kind=kOutput, calls=%fused_computation.107 | convolution fusion | flops 4294967296 | bytes 12582912 | tf_op jit(solution)/shard_map/dot_general | solution.py:47
  352.1 6.4 %collective-permute-done.21 = bf16[256,1536]{1,0:T(8,128)(2,1)S(1)} collective-permute-done((bf16[256,1536]{1,0:T(8,128)(2,1)S(1)}, bf16[256,1536]{1,0:T(8,128)(2,1)S(1)}, u32[]{:S(2)}, u32[]{:S(2)}) %collective-permute-start.21) | collective-permute-done | bytes 786464 | tf_op jit(solution)/shard_map/ppermute | solution.py:54
  358.6 17.2 %collective-permute-done.22 = bf16[256,1536]{1,0:T(8,128)(2,1)S(1)} collective-permute-done((bf16[256,1536]{1,0:T(8,128)(2,1)S(1)}, bf16[256,1536]{1,0:T(8,128)(2,1)S(1)}, u32[]{:S(2)}, u32[]{:S(2)}) %collective-permute-start.22) | collective-permute-done | bytes 786464 | tf_op jit(solution)/shard_map/ppermute | solution.py:54
  379.3 7.0 %convolution_bitcast_fusion = f32[1024,1536]{0,1:T(8,128)S(1)} fusion(bf16[2048,1536]{1,0:T(8,128)(2,1)S(1)} %constant_dynamic-update-slice_fusion.24, bf16[2048,1024]{1,0:T(8,128)(2,1)S(1)} %bitcast.133), kind=kOutput, calls=%fused_computation.16 | convolution fusion | flops 6442450944 | bytes 16777216 | tf_op jit(solution)/shard_map/dot_general | solution.py:47
  386.4 2.6 copy-done.4
  389.0 2.7 slice.105
  391.7 5.3 %copy.72 = f32[1024,1024]{1,0:T(8,128)} copy(f32[1024,1024]{0,1:T(8,128)} %slice.105) | data formatting | bytes 8388608
  397.0 1.7 fusion.19
  (163 shorter events, 40.4 us)
Async XLA Ops:
  7.2 86.5 %all-gather.3.cloned.1.call-start = ((), (), s32[]{:S(2)}) async-start(), calls=%async_computation.4 | async-start | bytes 5242880 | tf_op jit(solution)/shard_map/all_gather | solution.py:110
  9.5 187.4 %all-gather.5.cloned.1.call-start = ((), (), s32[]{:S(2)}) async-start(), calls=%async_computation.6 | async-start | bytes 5242880 | tf_op jit(solution)/shard_map/all_gather | solution.py:111
  93.6 15.7 %copy-start = (bf16[8192,1024]{1,0:T(8,128)(2,1)S(1)}, bf16[8192,1024]{1,0:T(8,128)(2,1)}, u32[]{:S(2)}) copy-start(bf16[8192,1024]{1,0:T(8,128)(2,1)} %param.10) | copy-start | bytes 50331652
  105.8 10.2 %copy-start.13 = (bf16[256,2048]{1,0:T(8,128)(2,1)S(1)}, bf16[256,2048]{1,0:T(8,128)(2,1)}, u32[]{:S(2)}) copy-start(bf16[256,2048]{1,0:T(8,128)(2,1)} %param.9) | copy-start | bytes 3145732
  105.8 17.2 %collective-permute-start = (bf16[256,512]{0,1:T(8,128)(2,1)}, bf16[256,512]{0,1:T(8,128)(2,1)}, u32[]{:S(2)}, u32[]{:S(2)}) collective-permute-start(bf16[256,512]{0,1:T(8,128)(2,1)} %get-tuple-element.57), channel_id=1, source_target_pairs={{0,8},{4,12},{8,0},{12,4},{16,24},{20,28},{24,16},{28,20},{1,9},{5... | collective-permute-start | bytes 786440 | tf_op jit(solution)/shard_map/ppermute | solution.py:54
  107.3 17.9 %collective-permute-start.1 = (bf16[256,512]{0,1:T(8,128)(2,1)}, bf16[256,512]{0,1:T(8,128)(2,1)}, u32[]{:S(2)}, u32[]{:S(2)}) collective-permute-start(bf16[256,512]{0,1:T(8,128)(2,1)} %get-tuple-element.57), channel_id=1, source_target_pairs={{0,16},{4,20},{8,24},{12,28},{16,0},{20,4},{24,8},{28,12},{1,17},{... | collective-permute-start | bytes 786440 | tf_op jit(solution)/shard_map/ppermute | solution.py:54
  108.8 18.2 %collective-permute-start.2 = (bf16[256,512]{0,1:T(8,128)(2,1)}, bf16[256,512]{0,1:T(8,128)(2,1)}, u32[]{:S(2)}, u32[]{:S(2)}) collective-permute-start(bf16[256,512]{0,1:T(8,128)(2,1)} %get-tuple-element.57), channel_id=1, source_target_pairs={{0,24},{4,28},{8,16},{12,20},{16,8},{20,12},{24,0},{28,4},{1,25},{... | collective-permute-start | bytes 786440 | tf_op jit(solution)/shard_map/ppermute | solution.py:54
  109.3 19.8 %collective-permute-start.3 = (bf16[256,512]{0,1:T(8,128)(2,1)}, bf16[256,512]{0,1:T(8,128)(2,1)}, u32[]{:S(2)}, u32[]{:S(2)}) collective-permute-start(bf16[256,512]{0,1:T(8,128)(2,1)} %get-tuple-element.57), channel_id=1, source_target_pairs={{0,4},{4,0},{8,12},{12,8},{16,20},{20,16},{24,28},{28,24},{1,5},{5... | collective-permute-start | bytes 786440 | tf_op jit(solution)/shard_map/ppermute | solution.py:54
  118.2 16.5 %copy-start.11 = (bf16[256,8,128]{2,0,1:T(8,128)(2,1)}, bf16[256,8,128]{2,0,1:T(8,128)(2,1)S(1)}, u32[]{:S(2)}) copy-start(bf16[256,8,128]{2,0,1:T(8,128)(2,1)S(1)} %copy.55) | copy-start | bytes 1572868
  118.2 53.7 %all-to-all-start = ((bf16[256,8,1024]{0,2,1:T(8,128)(2,1)}), bf16[256,8,1024]{0,2,1:T(8,128)(2,1)}, u32[]{:S(2)}, u32[]{:S(2)}) async-start(bf16[256,8,1024]{0,2,1:T(8,128)(2,1)} %bitcast.118), calls=%async_computation.1 | async-start | bytes 8388608 | tf_op jit(solution)/shard_map/all_to_all | solution.py:80
  122.7 278.6 %reduce-scatter.3.cloned.1.call-start = ((), (), s32[]{:S(2)}) async-start(), calls=%async_computation.5 | async-start | bytes 5242880 | tf_op jit(solution)/shard_map/reduce_scatter | solution.py:150
  123.0 7.8 %collective-permute-start.4 = (bf16[256,512]{0,1:T(8,128)(2,1)}, bf16[256,512]{0,1:T(8,128)(2,1)S(1)}, u32[]{:S(2)}, u32[]{:S(2)}) collective-permute-start(bf16[256,512]{0,1:T(8,128)(2,1)} %collective-permute-done), channel_id=1, source_target_pairs={{0,4},{4,0},{8,12},{12,8},{16,20},{20,16},{24,28},{28,24},{1,5},{5... | collective-permute-start | bytes 786440 | tf_op jit(solution)/shard_map/ppermute | solution.py:54
  125.2 6.3 %collective-permute-start.5 = (bf16[256,512]{0,1:T(8,128)(2,1)}, bf16[256,512]{0,1:T(8,128)(2,1)S(1)}, u32[]{:S(2)}, u32[]{:S(2)}) collective-permute-start(bf16[256,512]{0,1:T(8,128)(2,1)} %collective-permute-done.1), channel_id=1, source_target_pairs={{0,4},{4,0},{8,12},{12,8},{16,20},{20,16},{24,28},{28,24},{1,5},{5... | collective-permute-start | bytes 786440 | tf_op jit(solution)/shard_map/ppermute | solution.py:54
  127.0 5.3 %collective-permute-start.6 = (bf16[256,512]{0,1:T(8,128)(2,1)}, bf16[256,512]{0,1:T(8,128)(2,1)S(1)}, u32[]{:S(2)}, u32[]{:S(2)}) collective-permute-start(bf16[256,512]{0,1:T(8,128)(2,1)} %collective-permute-done.2), channel_id=1, source_target_pairs={{0,4},{4,0},{8,12},{12,8},{16,20},{20,16},{24,28},{28,24},{1,5},{5... | collective-permute-start | bytes 786440 | tf_op jit(solution)/shard_map/ppermute | solution.py:54
  134.6 9.4 %copy-start.7 = (bf16[2048,256]{0,1:T(8,128)(2,1)}, bf16[2048,256]{0,1:T(8,128)(2,1)S(1)}, u32[]{:S(2)}) copy-start(bf16[2048,256]{0,1:T(8,128)(2,1)S(1)} %get-tuple-element.47) | copy-start | bytes 3145732
  134.6 16.8 %copy-start.8 = (bf16[2048,256]{0,1:T(8,128)(2,1)}, bf16[2048,256]{0,1:T(8,128)(2,1)S(1)}, u32[]{:S(2)}) copy-start(bf16[2048,256]{0,1:T(8,128)(2,1)S(1)} %get-tuple-element.48) | copy-start | bytes 3145732
  144.1 11.7 %slice-start = ((s8[16777216]{0:T(1024)(128)(4,1)}), s8[4194304]{0:T(1024)(128)(4,1)S(1)}, s32[]{:S(2)}) async-start(s8[16777216]{0:T(1024)(128)(4,1)} %bitcast.119), calls=%async_computation.8 | async-start | bytes 8388608
  144.1 11.7 %slice-start.1 = ((s8[16777216]{0:T(1024)(128)(4,1)}), s8[4194304]{0:T(1024)(128)(4,1)S(1)}, s32[]{:S(2)}) async-start(s8[16777216]{0:T(1024)(128)(4,1)} %bitcast.119), calls=%async_computation.9 | async-start | bytes 8388608
  144.1 12.6 %slice-start.2 = ((s8[16777216]{0:T(1024)(128)(4,1)}), s8[4194304]{0:T(1024)(128)(4,1)S(1)}, s32[]{:S(2)}) async-start(s8[16777216]{0:T(1024)(128)(4,1)} %bitcast.119), calls=%async_computation.10 | async-start | bytes 8388608
  151.5 4.3 %copy-start.1 = (bf16[2,4,256,2048]{2,3,1,0:T(8,128)(2,1)}, bf16[2,4,256,2048]{2,3,1,0:T(8,128)(2,1)S(1)}, u32[]{:S(2)}) copy-start(bf16[2,4,256,2048]{2,3,1,0:T(8,128)(2,1)S(1)} %fusion.8) | copy-start | bytes 25165828
  151.5 6.6 %slice-start.3 = ((s8[16777216]{0:T(1024)(128)(4,1)}), s8[4194304]{0:T(1024)(128)(4,1)S(1)}, s32[]{:S(2)}) async-start(s8[16777216]{0:T(1024)(128)(4,1)} %bitcast.119), calls=%async_computation.11 | async-start | bytes 8388608
  208.9 53.7 %all-to-all-start.1 = ((bf16[256,8,1024]{0,2,1:T(8,128)(2,1)}), bf16[256,8,1024]{0,2,1:T(8,128)(2,1)}, u32[]{:S(2)}, u32[]{:S(2)}) async-start(bf16[256,8,1024]{0,2,1:T(8,128)(2,1)} %bitcast.135), calls=%async_computation.2 | async-start | bytes 8388608 | tf_op jit(solution)/shard_map/all_to_all | solution.py:80
  213.5 187.8 %reduce-scatter.5.cloned.1.call-start = ((), (), s32[]{:S(2)}) async-start(), calls=%async_computation.7 | async-start | bytes 5242880 | tf_op jit(solution)/shard_map/reduce_scatter | solution.py:176
  227.6 6.4 %copy-start.3 = (bf16[2,4,256,2048]{2,3,1,0:T(8,128)(2,1)S(1)}, bf16[2,4,256,2048]{2,3,1,0:T(8,128)(2,1)}, u32[]{:S(2)}) copy-start(bf16[2,4,256,2048]{2,3,1,0:T(8,128)(2,1)} %copy-done.2) | copy-start | bytes 25165828
  227.6 6.4 %copy-start.12 = (bf16[256,8,128]{2,0,1:T(8,128)(2,1)S(1)}, bf16[256,8,128]{2,0,1:T(8,128)(2,1)}, u32[]{:S(2)}) copy-start(bf16[256,8,128]{2,0,1:T(8,128)(2,1)} %copy-done.11) | copy-start | bytes 1572868
  269.8 3.2 collective-permute-start.8
  269.8 3.2 collective-permute-start.12
  270.3 2.7 collective-permute-start.10
  272.5 24.3 %collective-permute-start.7 = (bf16[256,512]{0,1:T(8,128)(2,1)}, bf16[256,512]{0,1:T(8,128)(2,1)S(1)}, u32[]{:S(2)}, u32[]{:S(2)}) collective-permute-start(bf16[256,512]{0,1:T(8,128)(2,1)} %get-tuple-element.40), channel_id=1, source_target_pairs={{0,4},{4,0},{8,12},{12,8},{16,20},{20,16},{24,28},{28,24},{1,5},{5... | collective-permute-start | bytes 786440 | tf_op jit(solution)/shard_map/ppermute | solution.py:54
  274.1 22.7 %collective-permute-start.13 = (bf16[256,512]{0,1:T(8,128)(2,1)}, bf16[256,512]{0,1:T(8,128)(2,1)}, u32[]{:S(2)}, u32[]{:S(2)}) collective-permute-start(bf16[256,512]{0,1:T(8,128)(2,1)} %get-tuple-element.45), channel_id=1, source_target_pairs={{0,24},{4,28},{8,16},{12,20},{16,8},{20,12},{24,0},{28,4},{1,25},{... | collective-permute-start | bytes 786440 | tf_op jit(solution)/shard_map/ppermute | solution.py:54
  274.7 22.1 %collective-permute-start.11 = (bf16[256,512]{0,1:T(8,128)(2,1)}, bf16[256,512]{0,1:T(8,128)(2,1)}, u32[]{:S(2)}, u32[]{:S(2)}) collective-permute-start(bf16[256,512]{0,1:T(8,128)(2,1)} %get-tuple-element.46), channel_id=1, source_target_pairs={{0,16},{4,20},{8,24},{12,28},{16,0},{20,4},{24,8},{28,12},{1,17},{... | collective-permute-start | bytes 786440 | tf_op jit(solution)/shard_map/ppermute | solution.py:54
  276.0 20.7 %collective-permute-start.9 = (bf16[256,512]{0,1:T(8,128)(2,1)}, bf16[256,512]{0,1:T(8,128)(2,1)}, u32[]{:S(2)}, u32[]{:S(2)}) collective-permute-start(bf16[256,512]{0,1:T(8,128)(2,1)} %get-tuple-element.44), channel_id=1, source_target_pairs={{0,8},{4,12},{8,0},{12,4},{16,24},{20,28},{24,16},{28,20},{1,9},{5... | collective-permute-start | bytes 786440 | tf_op jit(solution)/shard_map/ppermute | solution.py:54
  298.0 6.2 %copy-start.10 = (f32[256,512]{0,1:T(8,128)}, f32[256,512]{0,1:T(8,128)S(1)}, u32[]{:S(2)}) copy-start(f32[256,512]{0,1:T(8,128)S(1)} %convert_add_fusion) | copy-start | bytes 1572868
  298.1 6.1 %copy-start.9 = (bf16[8192,256]{1,0:T(8,128)(2,1)S(1)}, bf16[8192,256]{1,0:T(8,128)(2,1)}, u32[]{:S(2)}) copy-start(bf16[8192,256]{1,0:T(8,128)(2,1)} %param.12) | copy-start | bytes 12582916
  307.6 14.9 %collective-permute-start.14 = (bf16[256,1024]{0,1:T(8,128)(2,1)S(1)}, bf16[256,1024]{0,1:T(8,128)(2,1)S(1)}, u32[]{:S(2)}, u32[]{:S(2)}) collective-permute-start(bf16[256,1024]{0,1:T(8,128)(2,1)S(1)} %bitcast.123), channel_id=1, source_target_pairs={{0,8},{4,12},{8,0},{12,4},{16,24},{20,28},{24,16},{28,20},{1,9},{5... | collective-permute-start | bytes 1572872 | tf_op jit(solution)/shard_map/ppermute | solution.py:54
  308.1 24.0 %collective-permute-start.15 = (bf16[256,1024]{0,1:T(8,128)(2,1)S(1)}, bf16[256,1024]{0,1:T(8,128)(2,1)S(1)}, u32[]{:S(2)}, u32[]{:S(2)}) collective-permute-start(bf16[256,1024]{0,1:T(8,128)(2,1)S(1)} %bitcast.124), channel_id=1, source_target_pairs={{0,16},{4,20},{8,24},{12,28},{16,0},{20,4},{24,8},{28,12},{1,17},{... | collective-permute-start | bytes 1572872 | tf_op jit(solution)/shard_map/ppermute | solution.py:54
  308.8 23.4 %collective-permute-start.16 = (bf16[256,1024]{0,1:T(8,128)(2,1)S(1)}, bf16[256,1024]{0,1:T(8,128)(2,1)S(1)}, u32[]{:S(2)}, u32[]{:S(2)}) collective-permute-start(bf16[256,1024]{0,1:T(8,128)(2,1)S(1)} %bitcast.125), channel_id=1, source_target_pairs={{0,24},{4,28},{8,16},{12,20},{16,8},{20,12},{24,0},{28,4},{1,25},{... | collective-permute-start | bytes 1572872 | tf_op jit(solution)/shard_map/ppermute | solution.py:54
  311.1 21.8 %collective-permute-start.17 = (bf16[256,1024]{0,1:T(8,128)(2,1)S(1)}, bf16[256,1024]{0,1:T(8,128)(2,1)S(1)}, u32[]{:S(2)}, u32[]{:S(2)}) collective-permute-start(bf16[256,1024]{0,1:T(8,128)(2,1)S(1)} %bitcast.126), channel_id=1, source_target_pairs={{0,4},{4,0},{8,12},{12,8},{16,20},{20,16},{24,28},{28,24},{1,5},{5... | collective-permute-start | bytes 1572872 | tf_op jit(solution)/shard_map/ppermute | solution.py:54
  322.5 10.6 %collective-permute-start.18 = (bf16[256,1024]{0,1:T(8,128)(2,1)S(1)}, bf16[256,1024]{0,1:T(8,128)(2,1)S(1)}, u32[]{:S(2)}, u32[]{:S(2)}) collective-permute-start(bf16[256,1024]{0,1:T(8,128)(2,1)S(1)} %collective-permute-done.14), channel_id=1, source_target_pairs={{0,4},{4,0},{8,12},{12,8},{16,20},{20,16},{24,28},{28,24},{1,5},{5... | collective-permute-start | bytes 1572872 | tf_op jit(solution)/shard_map/ppermute | solution.py:54
  332.2 1.9 collective-permute-start.19
  332.2 2.6 collective-permute-start.20
  338.1 20.4 %collective-permute-start.21 = (bf16[256,1536]{1,0:T(8,128)(2,1)S(1)}, bf16[256,1536]{1,0:T(8,128)(2,1)S(1)}, u32[]{:S(2)}, u32[]{:S(2)}) collective-permute-start(bf16[256,1536]{1,0:T(8,128)(2,1)S(1)} %pad_maximum_fusion.1), channel_id=1, source_target_pairs={{0,8},{4,12},{8,0},{12,4},{16,24},{20,28},{24,16},{28,20},{1,9},{5... | collective-permute-start | bytes 2359304 | tf_op jit(solution)/shard_map/ppermute | solution.py:54
  339.7 36.2 %collective-permute-start.22 = (bf16[256,1536]{1,0:T(8,128)(2,1)S(1)}, bf16[256,1536]{1,0:T(8,128)(2,1)S(1)}, u32[]{:S(2)}, u32[]{:S(2)}) collective-permute-start(bf16[256,1536]{1,0:T(8,128)(2,1)S(1)} %pad_maximum_fusion.1), channel_id=1, source_target_pairs={{0,16},{4,20},{8,24},{12,28},{16,0},{20,4},{24,8},{28,12},{1,17},{... | collective-permute-start | bytes 2359304 | tf_op jit(solution)/shard_map/ppermute | solution.py:54
  340.2 35.7 %collective-permute-start.23 = (bf16[256,1536]{1,0:T(8,128)(2,1)S(1)}, bf16[256,1536]{1,0:T(8,128)(2,1)S(1)}, u32[]{:S(2)}, u32[]{:S(2)}) collective-permute-start(bf16[256,1536]{1,0:T(8,128)(2,1)S(1)} %pad_maximum_fusion.1), channel_id=1, source_target_pairs={{0,24},{4,28},{8,16},{12,20},{16,8},{20,12},{24,0},{28,4},{1,25},{... | collective-permute-start | bytes 2359304 | tf_op jit(solution)/shard_map/ppermute | solution.py:54
  351.6 24.9 %collective-permute-start.24 = (bf16[256,1536]{1,0:T(8,128)(2,1)S(1)}, bf16[256,1536]{1,0:T(8,128)(2,1)S(1)}, u32[]{:S(2)}, u32[]{:S(2)}) collective-permute-start(bf16[256,1536]{1,0:T(8,128)(2,1)S(1)} %pad_maximum_fusion.1), channel_id=1, source_target_pairs={{0,4},{4,0},{8,12},{12,8},{16,20},{20,16},{24,28},{28,24},{1,5},{5... | collective-permute-start | bytes 2359304 | tf_op jit(solution)/shard_map/ppermute | solution.py:54
  358.6 18.1 %collective-permute-start.25 = (bf16[256,1536]{1,0:T(8,128)(2,1)S(1)}, bf16[256,1536]{1,0:T(8,128)(2,1)S(1)}, u32[]{:S(2)}, u32[]{:S(2)}) collective-permute-start(bf16[256,1536]{1,0:T(8,128)(2,1)S(1)} %collective-permute-done.21), channel_id=1, source_target_pairs={{0,4},{4,0},{8,12},{12,8},{16,20},{20,16},{24,28},{28,24},{1,5},{5... | collective-permute-start | bytes 2359304 | tf_op jit(solution)/shard_map/ppermute | solution.py:54
  375.8 2.3 collective-permute-start.26
  375.9 3.3 collective-permute-start.27
  (4 other events, 11.4 us)
Sparse Core Ops, SparseCore 0:
  10.1 83.4 all-gather.2
  117.5 79.4 all-gather.4
  199.8 75.2 reduce-scatter.2
  307.7 73.5 reduce-scatter.4

commit v2 on v1

--- a/solution.py
+++ b/solution.py
@@ -147,9 +147,9 @@
     )
     heads = heads4.reshape(tok_rows, -1)
     out_part = jnp.dot(heads, w_output, preferred_element_type=f32).astype(bf16)
+    out_part, full_grad = lax.optimization_barrier((out_part, full_grad))
     layer_out = lax.psum_scatter(out_part, "tensor", scatter_dimension=1, tiled=True)
 
-    full_grad = after(full_grad, out_part)
     g_cols = reshard_columns(full_grad)
     heads_all = in_order(gather_blocks(heads), me)
     grad_heads = after(contract_last(full_grad, w_output).astype(bf16), x_cols)
@@ -165,8 +165,8 @@
     kv_part = jnp.concatenate(
         [key_part.reshape(all_rows, -1), value_part.reshape(all_rows, -1)], 1
     ).astype(bf16)
-    kv_part = after(kv_part, g_cols)
     kv_grad = scatter_sum([kv_part[k * tok_rows : (k + 1) * tok_rows] for k in range(seq_count)])
+    kv_grad = after(kv_grad, g_cols)
     pre_q = rotate_back(query_grad.reshape(tok_rows, -1), cosine, sine, HD).astype(bf16)
     pre_k = rotate_back(kv_grad[:, :k_width], cosine, sine, HD).astype(bf16)
     pre_v = kv_grad[:, k_width:].astype(bf16)

time: 416 us -> 399 us (0.959)
  waiting for transfers between devices: 175 us -> 157 us
    all_to_all x2, waiting for transfers between devices: 32.8 us -> 7.27 us  [reshard_columns(): return lax.all_to_all(full, 'seq', 1, 0, tiled=True)]
    ppermute x28, waiting for transfers between devices: 48.2 us -> 55.4 us  [swap(): return lax.ppermute(value, 'seq', [(i, i ^ step) for i in range(count)])]
    unnamed x57 -> x59, local copies, waits for them, and re-layouts: 36.6 us -> 36.6 us
  transfers between devices with their start and end apart: 34 -> 34, of which waited for: 12 -> 16; matrix products, arithmetic and copies ran while one was open for 41% -> 43% of each run, Pallas kernels for 0% -> 0%
where the time goes in v2:
time: 399 us; the launch traced here: 391 us
  waiting for transfers between devices  157 us (39%)
  matrix products  116 us (29%)
  local copies, waits for them, and re-layouts  61.1 us (15%)
  starting transfers between devices  26.8 us (7%)
  other arithmetic  15.5 us (4%)
  between operations  15.5 us (4%)
    all_gather x1, waiting for transfers between devices, on_device(): full_x = lax.all_gather(tokens, 'tensor', axis=1, tiled=True)  75.2 us
    ppermute x28, waiting for transfers between devices, swap(): return lax.ppermute(value, 'seq', [(i, i ^ step) for i in range(count)])  55.4 us
    dot_general x4, matrix products, contract_last(): lax.dot_general(left, right, (((1,), (1,)), ((), ())), preferred_element_...  40.2 us
    unnamed x59, local copies, waits for them, and re-layouts  36.6 us
    all_gather x1, waiting for transfers between devices, on_device(): lax.all_gather(after(cotangent, full_x), 'tensor', axis=1, tiled=True)  18.6 us
    ppermute x28, starting transfers between devices, swap(): return lax.ppermute(value, 'seq', [(i, i ^ step) for i in range(count)])  17.3 us
    dot_general x2, matrix products, contract_first(): lax.dot_general(left, right, (((0,), (0,)), ((), ())), preferred_element_...  17 us
    all_to_all x2, local copies, waits for them, and re-layouts, reshard_columns(): return lax.all_to_all(full, 'seq', 1, 0, tiled=True)  13.1 us
  transfers between devices with their start and end apart: 34, of which 16 were waited for; matrix products, arithmetic and copies ran while one was open for 43% of the time, Pallas kernels for 0%

profile of v2, /device:TPU:0, one launch (start us, length us, event | category | flops | bytes accessed | tf_op | source)
XLA Modules:
  0.0 391.3 jit_solution(18014868370837950092)
XLA Ops:
  7.2 2.3 copy.52
  17.1 1.4 compare_and_fusion
  18.5 75.2 %all-gather.3.cloned.1.call-done = bf16[256,8192]{0,1:T(8,128)(2,1)} async-done(((bf16[256,2048]{0,1:T(8,128)(2,1)}), bf16[256,8192]{0,1:T(8,128)(2,1)}) %all-gather.3.cloned.1.call-update) | async-done | bytes 4194320 | tf_op jit(solution)/shard_map/all_gather | solution.py:110
  93.6 5.3 %fusion.31 = f32[256,256]{0,1:T(8,128)S(1)} fusion(bf16[256,8192]{0,1:T(8,128)(2,1)} %all-gather.3.cloned.1.call-done, bf16[8192,256]{1,0:T(8,128)(2,1)} %param.11), kind=kOutput, calls=%fused_computation.126 | convolution fusion | flops 1073741824 | bytes 8650752 | tf_op jit(solution)/shard_map/dot_general | solution.py:116
  99.0 5.9 %convolution_convert_fusion.3 = bf16[256,256]{0,1:T(8,128)(2,1)S(1)} fusion(bf16[256,8192]{0,1:T(8,128)(2,1)} %all-gather.3.cloned.1.call-done, bf16[8192,256]{1,0:T(8,128)(2,1)} %param.12), kind=kOutput, calls=%fused_computation.42 | convolution fusion | flops 1073807360 | bytes 8519680 | tf_op jit(solution)/shard_map/dot_general | solution.py:117
  105.8 1.5 collective-permute-start
  107.3 1.5 collective-permute-start.1
  109.3 6.5 %convolution_bitcast_fusion.3 = f32[32,8,8,128]{3,1,2,0:T(8,128)S(1)} fusion(bf16[256,8192]{0,1:T(8,128)(2,1)} %all-gather.3.cloned.1.call-done, bf16[8192,1024]{1,0:T(8,128)(2,1)S(1)} %copy-done), kind=kOutput, calls=%fused_computation.38 | convolution fusion | flops 4294967296 | bytes 22020096 | tf_op jit(solution)/shard_map/dot_general | solution.py:123
  118.2 4.6 %all-to-all-start = ((bf16[256,8,1024]{0,2,1:T(8,128)(2,1)}), bf16[256,8,1024]{0,2,1:T(8,128)(2,1)}, u32[]{:S(2)}, u32[]{:S(2)}) async-start(bf16[256,8,1024]{0,2,1:T(8,128)(2,1)} %bitcast.118), calls=%async_computation.1 | async-start | bytes 8388608 | tf_op jit(solution)/shard_map/all_to_all | solution.py:80
  123.5 1.7 constant_dynamic-update-slice_fusion.6
  125.3 1.7 constant_dynamic-update-slice_fusion.5
  127.4 1.7 constant_dynamic-update-slice_fusion.4
  129.1 1.7 constant_dynamic-update-slice_fusion.3
  133.0 1.7 fusion.27
  134.7 9.4 %fusion.29 = (f32[2,4,256]{2,1,0:T(4,128)S(1)}, f32[2,4,256,2048]{2,3,1,0:T(8,128)}) fusion(pred[256,2048]{0,1:T(8,128)(4,1)S(1)} %compare_and_fusion, bf16[2048,2,128,1]{0,2,3,1:T(8,128)(2,1)S(1)} %bitcast.142, bf16[256,2,4,128]{3,0,2,1:T(8,128)(2,1)S(1)} %bitcast.147), kind=kOutput, calls=%fused_computation.124 | convolution fusion | flops 1090521088 | bytes 18882560 | tf_op jit(solution)/shard_map/sub | solution.py:142
  144.1 7.4 %fusion.8 = bf16[2,4,256,2048]{2,3,1,0:T(8,128)(2,1)S(1)} fusion(f32[2,4,256,2048]{2,3,1,0:T(8,128)} %get-tuple-element.64, f32[2,4,256]{2,1,0:T(4,128)S(1)} %get-tuple-element.63), kind=kLoop, calls=%fused_computation.15 | loop fusion | flops 8388608 | bytes 25174016 | tf_op jit(solution)/shard_map/convert_element_type | solution.py:144
  152.7 3.0 copy-done.1
  156.6 1.5 slice-done.3
  158.1 6.5 %convolution_convert_fusion = bf16[256,8192]{1,0:T(8,128)(2,1)} fusion(bf16[256,1024]{0,1:T(8,128)(2,1)S(1)} %bitcast.128, bf16[1024,8192]{1,0:T(8,128)(2,1)S(1)} %bitcast.126), kind=kOutput, calls=%fused_computation.9 | convolution fusion | flops 4297064448 | bytes 21495808 | tf_op jit(solution)/shard_map/dot_general | solution.py:149
  164.6 7.3 %all-to-all-done = bf16[256,8,1024]{0,2,1:T(8,128)(2,1)} async-done(((bf16[256,8,1024]{0,2,1:T(8,128)(2,1)}), bf16[256,8,1024]{0,2,1:T(8,128)(2,1)}, u32[]{:S(2)}, u32[]{:S(2)}) %all-to-all-start) | async-done | bytes 4194336 | tf_op jit(solution)/shard_map/all_to_all | solution.py:80
  171.9 6.4 %copy.59 = bf16[8,256,1024]{2,1,0:T(8,128)(2,1)} copy(bf16[8,256,1024]{1,2,0:T(8,128)(2,1)} %bitcast.16) | data formatting | bytes 8388608 | tf_op jit(solution)/shard_map/all_to_all | solution.py:80
  178.3 18.6 %all-gather.5.cloned.1.call-done = bf16[256,8192]{0,1:T(8,128)(2,1)} async-done(((bf16[256,2048]{0,1:T(8,128)(2,1)}), bf16[256,8192]{0,1:T(8,128)(2,1)}) %all-gather.5.cloned.1.call-update) | async-done | bytes 4194320 | tf_op jit(solution)/shard_map/all_gather | solution.py:111
  197.0 11.6 %convolution_convert_fusion.2 = bf16[256,1024]{1,0:T(8,128)(2,1)S(1)} fusion(bf16[256,8192]{0,1:T(8,128)(2,1)} %all-gather.5.cloned.1.call-done, bf16[1024,8192]{1,0:T(8,128)(2,1)} %param.13), kind=kOutput, calls=%fused_computation.41 | convolution fusion | flops 4295229440 | bytes 21495808 | tf_op jit(solution)/shard_map/dot_general | solution.py:41
  208.8 4.6 %all-to-all-start.1 = ((bf16[256,8,1024]{0,2,1:T(8,128)(2,1)}), bf16[256,8,1024]{0,2,1:T(8,128)(2,1)}, u32[]{:S(2)}, u32[]{:S(2)}) async-start(bf16[256,8,1024]{0,2,1:T(8,128)(2,1)} %bitcast.140), calls=%async_computation.2 | async-start | bytes 8388608 | tf_op jit(solution)/shard_map/all_to_all | solution.py:80
  213.6 8.0 %fusion.2 = bf16[2,4,256,2048]{2,3,1,0:T(8,128)(2,1)S(1)} fusion(f32[2,4,256]{2,1,0:T(4,128)S(1)} %bitcast.154, f32[2,4,256,2048]{2,3,1,0:T(8,128)} %get-tuple-element.64, f32[2,4,256]{2,1,0:T(4,128)S(1)} %get-tuple-element.63, bf16[2048,2,128,1]{0,2,3,1:T(8,128)(2,1)} %bitcast.145, bf16[256,2,4,128]{0,3,2,1:T(8,128)(2,1)S(1)} %bitcast.136), kind=kOutput, calls=%fused_computation.3 | convolution fusion | flops 1090519040 | bytes 26755072 | tf_op jit(solution)/shard_map/igrd,jgd->grij/dot_general | solution.py:158
  221.6 3.3 convolution_multiply_fusion
  227.6 6.2 %fusion.12 = bf16[2,128,2048]{2,1,0:T(8,128)(2,1)S(1)} fusion(bf16[256,2,4,128]{3,0,2,1:T(8,128)(2,1)S(1)} %bitcast.148, bf16[2,4,256,2048]{2,3,1,0:T(8,128)(2,1)} %copy-done.2), kind=kOutput, calls=%fused_computation.35 | convolution fusion | flops 1074790400 | bytes 9961472 | tf_op jit(solution)/shard_map/grij,igrd->jgd/dot_general | solution.py:163
  233.9 6.3 %fusion.13 = bf16[2,128,2048]{2,1,0:T(8,128)(2,1)S(1)} fusion(bf16[256,2,4,128]{0,3,2,1:T(8,128)(2,1)S(1)} %bitcast.137, bf16[2,4,256,2048]{2,3,1,0:T(8,128)(2,1)} %copy-done.1), kind=kOutput, calls=%fused_computation.36 | convolution fusion | flops 1074266112 | bytes 9961472 | tf_op jit(solution)/shard_map/grij,igrd->jgd/dot_general | solution.py:164
  244.6 2.8 collective-permute-start.13
  248.1 19.1 %fusion.25 = f32[256,8192]{1,0:T(8,128)} fusion(bf16[8192,1024]{1,0:T(8,128)(2,1)} %param.10, bf16[32,8,8,128]{3,2,1,0:T(8,128)(2,1)S(1)} %bitcast.134), kind=kOutput, calls=%fused_computation.120 | convolution fusion | flops 4294967296 | bytes 25690112 | tf_op jit(solution)/shard_map/dot_general | solution.py:41
  268.5 4.2 %collective-permute-done.11 = bf16[256,512]{0,1:T(8,128)(2,1)} collective-permute-done((bf16[256,512]{0,1:T(8,128)(2,1)}, bf16[256,512]{0,1:T(8,128)(2,1)}, u32[]{:S(2)}, u32[]{:S(2)}) %collective-permute-start.11) | collective-permute-done | bytes 262176 | tf_op jit(solution)/shard_map/ppermute | solution.py:54
  272.8 2.1 convert_add_fusion
  274.9 6.7 %copy.69 = bf16[8,256,1024]{2,1,0:T(8,128)(2,1)} copy(bf16[8,256,1024]{1,2,0:T(8,128)(2,1)} %bitcast.35) | data formatting | bytes 8388608 | tf_op jit(solution)/shard_map/all_to_all | solution.py:80
  281.7 6.1 %convolution_add_fusion.1 = f32[256,8192]{1,0:T(8,128)S(1)} fusion(f32[256,8192]{1,0:T(8,128)} %fusion.25, bf16[256,256]{0,1:T(8,128)(2,1)S(1)} %bitcast.150, bf16[8192,256]{1,0:T(8,128)(2,1)} %param.11), kind=kOutput, calls=%fused_computation.8 | convolution fusion | flops 1075838976 | bytes 21102592 | tf_op jit(solution)/shard_map/dot_general | solution.py:41
  287.8 3.4 fusion.4
  291.2 1.5 collective-permute-start.14
  294.8 11.3 %collective-permute-done.14 = bf16[256,1024]{0,1:T(8,128)(2,1)S(1)} collective-permute-done((bf16[256,1024]{0,1:T(8,128)(2,1)S(1)}, bf16[256,1024]{0,1:T(8,128)(2,1)S(1)}, u32[]{:S(2)}, u32[]{:S(2)}) %collective-permute-start.14) | collective-permute-done | bytes 524320 | tf_op jit(solution)/shard_map/ppermute | solution.py:54
  306.7 10.8 %collective-permute-done.15 = bf16[256,1024]{0,1:T(8,128)(2,1)S(1)} collective-permute-done((bf16[256,1024]{0,1:T(8,128)(2,1)S(1)}, bf16[256,1024]{0,1:T(8,128)(2,1)S(1)}, u32[]{:S(2)}, u32[]{:S(2)}) %collective-permute-start.15) | collective-permute-done | bytes 524320 | tf_op jit(solution)/shard_map/ppermute | solution.py:54
  320.4 1.9 copy-done.5
  323.6 2.5 collective-permute-start.23
  326.1 10.0 %fusion.32 = f32[1024,1024]{1,0:T(8,128)} fusion(bf16[2048,1024]{0,1:T(8,128)(2,1)} %copy-done.5, bf16[2048,1024]{1,0:T(8,128)(2,1)} %bitcast.141), kind=kOutput, calls=%fused_computation.127 | convolution fusion | flops 4294967296 | bytes 12582912 | tf_op jit(solution)/shard_map/dot_general | solution.py:47
  336.6 6.4 %collective-permute-done.21 = bf16[256,1536]{1,0:T(8,128)(2,1)S(1)} collective-permute-done((bf16[256,1536]{1,0:T(8,128)(2,1)S(1)}, bf16[256,1536]{1,0:T(8,128)(2,1)S(1)}, u32[]{:S(2)}, u32[]{:S(2)}) %collective-permute-start.21) | collective-permute-done | bytes 786464 | tf_op jit(solution)/shard_map/ppermute | solution.py:54
  343.1 16.1 %collective-permute-done.22 = bf16[256,1536]{1,0:T(8,128)(2,1)S(1)} collective-permute-done((bf16[256,1536]{1,0:T(8,128)(2,1)S(1)}, bf16[256,1536]{1,0:T(8,128)(2,1)S(1)}, u32[]{:S(2)}, u32[]{:S(2)}) %collective-permute-start.22) | collective-permute-done | bytes 786464 | tf_op jit(solution)/shard_map/ppermute | solution.py:54
  362.6 7.1 %convolution_bitcast_fusion = f32[1024,1536]{0,1:T(8,128)S(1)} fusion(bf16[2048,1536]{1,0:T(8,128)(2,1)S(1)} %constant_dynamic-update-slice_fusion.24, bf16[2048,1024]{1,0:T(8,128)(2,1)S(1)} %bitcast.139), kind=kOutput, calls=%fused_computation.16 | convolution fusion | flops 6442450944 | bytes 16777216 | tf_op jit(solution)/shard_map/dot_general | solution.py:47
  369.7 2.6 copy-done.3
  372.3 2.6 slice.118
  374.9 5.3 %copy.72 = f32[1024,1024]{1,0:T(8,128)} copy(f32[1024,1024]{0,1:T(8,128)} %slice.118) | data formatting | bytes 8388608
  380.3 1.7 fusion.26
  (165 shorter events, 39.1 us)
Async XLA Ops:
  7.2 86.5 %all-gather.3.cloned.1.call-start = ((), (), s32[]{:S(2)}) async-start(), calls=%async_computation.4 | async-start | bytes 5242880 | tf_op jit(solution)/shard_map/all_gather | solution.py:110
  9.5 187.4 %all-gather.5.cloned.1.call-start = ((), (), s32[]{:S(2)}) async-start(), calls=%async_computation.5 | async-start | bytes 5242880 | tf_op jit(solution)/shard_map/all_gather | solution.py:111
  93.6 15.7 %copy-start = (bf16[8192,1024]{1,0:T(8,128)(2,1)S(1)}, bf16[8192,1024]{1,0:T(8,128)(2,1)}, u32[]{:S(2)}) copy-start(bf16[8192,1024]{1,0:T(8,128)(2,1)} %param.10) | copy-start | bytes 50331652
  105.8 10.2 %copy-start.14 = (bf16[256,2048]{1,0:T(8,128)(2,1)S(1)}, bf16[256,2048]{1,0:T(8,128)(2,1)}, u32[]{:S(2)}) copy-start(bf16[256,2048]{1,0:T(8,128)(2,1)} %param.9) | copy-start | bytes 3145732
  105.8 17.2 %collective-permute-start = (bf16[256,512]{0,1:T(8,128)(2,1)}, bf16[256,512]{0,1:T(8,128)(2,1)}, u32[]{:S(2)}, u32[]{:S(2)}) collective-permute-start(bf16[256,512]{0,1:T(8,128)(2,1)} %get-tuple-element.59), channel_id=1, source_target_pairs={{0,8},{4,12},{8,0},{12,4},{16,24},{20,28},{24,16},{28,20},{1,9},{5... | collective-permute-start | bytes 786440 | tf_op jit(solution)/shard_map/ppermute | solution.py:54
  107.3 17.9 %collective-permute-start.1 = (bf16[256,512]{0,1:T(8,128)(2,1)}, bf16[256,512]{0,1:T(8,128)(2,1)}, u32[]{:S(2)}, u32[]{:S(2)}) collective-permute-start(bf16[256,512]{0,1:T(8,128)(2,1)} %get-tuple-element.59), channel_id=1, source_target_pairs={{0,16},{4,20},{8,24},{12,28},{16,0},{20,4},{24,8},{28,12},{1,17},{... | collective-permute-start | bytes 786440 | tf_op jit(solution)/shard_map/ppermute | solution.py:54
  108.8 18.2 %collective-permute-start.2 = (bf16[256,512]{0,1:T(8,128)(2,1)}, bf16[256,512]{0,1:T(8,128)(2,1)}, u32[]{:S(2)}, u32[]{:S(2)}) collective-permute-start(bf16[256,512]{0,1:T(8,128)(2,1)} %get-tuple-element.59), channel_id=1, source_target_pairs={{0,24},{4,28},{8,16},{12,20},{16,8},{20,12},{24,0},{28,4},{1,25},{... | collective-permute-start | bytes 786440 | tf_op jit(solution)/shard_map/ppermute | solution.py:54
  109.3 19.8 %collective-permute-start.3 = (bf16[256,512]{0,1:T(8,128)(2,1)}, bf16[256,512]{0,1:T(8,128)(2,1)}, u32[]{:S(2)}, u32[]{:S(2)}) collective-permute-start(bf16[256,512]{0,1:T(8,128)(2,1)} %get-tuple-element.59), channel_id=1, source_target_pairs={{0,4},{4,0},{8,12},{12,8},{16,20},{20,16},{24,28},{28,24},{1,5},{5... | collective-permute-start | bytes 786440 | tf_op jit(solution)/shard_map/ppermute | solution.py:54
  118.2 16.5 %copy-start.12 = (bf16[256,8,128]{2,0,1:T(8,128)(2,1)}, bf16[256,8,128]{2,0,1:T(8,128)(2,1)S(1)}, u32[]{:S(2)}) copy-start(bf16[256,8,128]{2,0,1:T(8,128)(2,1)S(1)} %copy.55) | copy-start | bytes 1572868
  118.2 53.7 %all-to-all-start = ((bf16[256,8,1024]{0,2,1:T(8,128)(2,1)}), bf16[256,8,1024]{0,2,1:T(8,128)(2,1)}, u32[]{:S(2)}, u32[]{:S(2)}) async-start(bf16[256,8,1024]{0,2,1:T(8,128)(2,1)} %bitcast.118), calls=%async_computation.1 | async-start | bytes 8388608 | tf_op jit(solution)/shard_map/all_to_all | solution.py:80
  122.8 261.8 %reduce-scatter.3.cloned.1.call-start = ((), (), s32[]{:S(2)}) async-start(), calls=%async_computation.6 | async-start | bytes 5242880 | tf_op jit(solution)/shard_map/reduce_scatter | solution.py:151
  123.0 7.8 %collective-permute-start.4 = (bf16[256,512]{0,1:T(8,128)(2,1)}, bf16[256,512]{0,1:T(8,128)(2,1)S(1)}, u32[]{:S(2)}, u32[]{:S(2)}) collective-permute-start(bf16[256,512]{0,1:T(8,128)(2,1)} %collective-permute-done), channel_id=1, source_target_pairs={{0,4},{4,0},{8,12},{12,8},{16,20},{20,16},{24,28},{28,24},{1,5},{5... | collective-permute-start | bytes 786440 | tf_op jit(solution)/shard_map/ppermute | solution.py:54
  125.2 6.3 %collective-permute-start.5 = (bf16[256,512]{0,1:T(8,128)(2,1)}, bf16[256,512]{0,1:T(8,128)(2,1)S(1)}, u32[]{:S(2)}, u32[]{:S(2)}) collective-permute-start(bf16[256,512]{0,1:T(8,128)(2,1)} %collective-permute-done.1), channel_id=1, source_target_pairs={{0,4},{4,0},{8,12},{12,8},{16,20},{20,16},{24,28},{28,24},{1,5},{5... | collective-permute-start | bytes 786440 | tf_op jit(solution)/shard_map/ppermute | solution.py:54
  127.0 5.3 %collective-permute-start.6 = (bf16[256,512]{0,1:T(8,128)(2,1)}, bf16[256,512]{0,1:T(8,128)(2,1)S(1)}, u32[]{:S(2)}, u32[]{:S(2)}) collective-permute-start(bf16[256,512]{0,1:T(8,128)(2,1)} %collective-permute-done.2), channel_id=1, source_target_pairs={{0,4},{4,0},{8,12},{12,8},{16,20},{20,16},{24,28},{28,24},{1,5},{5... | collective-permute-start | bytes 786440 | tf_op jit(solution)/shard_map/ppermute | solution.py:54
  134.6 9.4 %copy-start.6 = (bf16[2048,256]{0,1:T(8,128)(2,1)}, bf16[2048,256]{0,1:T(8,128)(2,1)S(1)}, u32[]{:S(2)}) copy-start(bf16[2048,256]{0,1:T(8,128)(2,1)S(1)} %get-tuple-element.49) | copy-start | bytes 3145732
  134.6 16.8 %copy-start.7 = (bf16[2048,256]{0,1:T(8,128)(2,1)}, bf16[2048,256]{0,1:T(8,128)(2,1)S(1)}, u32[]{:S(2)}) copy-start(bf16[2048,256]{0,1:T(8,128)(2,1)S(1)} %get-tuple-element.50) | copy-start | bytes 3145732
  144.1 11.7 %slice-start = ((s8[16777216]{0:T(1024)(128)(4,1)}), s8[4194304]{0:T(1024)(128)(4,1)S(1)}, s32[]{:S(2)}) async-start(s8[16777216]{0:T(1024)(128)(4,1)} %bitcast.125), calls=%async_computation.8 | async-start | bytes 8388608
  144.1 11.7 %slice-start.1 = ((s8[16777216]{0:T(1024)(128)(4,1)}), s8[4194304]{0:T(1024)(128)(4,1)S(1)}, s32[]{:S(2)}) async-start(s8[16777216]{0:T(1024)(128)(4,1)} %bitcast.125), calls=%async_computation.9 | async-start | bytes 8388608
  144.1 12.5 %slice-start.2 = ((s8[16777216]{0:T(1024)(128)(4,1)}), s8[4194304]{0:T(1024)(128)(4,1)S(1)}, s32[]{:S(2)}) async-start(s8[16777216]{0:T(1024)(128)(4,1)} %bitcast.125), calls=%async_computation.10 | async-start | bytes 8388608
  151.5 6.6 %slice-start.3 = ((s8[16777216]{0:T(1024)(128)(4,1)}), s8[4194304]{0:T(1024)(128)(4,1)S(1)}, s32[]{:S(2)}) async-start(s8[16777216]{0:T(1024)(128)(4,1)} %bitcast.125), calls=%async_computation.11 | async-start | bytes 8388608
  208.8 66.1 %all-to-all-start.1 = ((bf16[256,8,1024]{0,2,1:T(8,128)(2,1)}), bf16[256,8,1024]{0,2,1:T(8,128)(2,1)}, u32[]{:S(2)}, u32[]{:S(2)}) async-start(bf16[256,8,1024]{0,2,1:T(8,128)(2,1)} %bitcast.140), calls=%async_computation.2 | async-start | bytes 8388608 | tf_op jit(solution)/shard_map/all_to_all | solution.py:80
  213.4 171.2 %reduce-scatter.5.cloned.1.call-start = ((), (), s32[]{:S(2)}) async-start(), calls=%async_computation.7 | async-start | bytes 5242880 | tf_op jit(solution)/shard_map/reduce_scatter | solution.py:176
  233.8 8.2 %copy-start.8 = (f32[256,8,64]{2,1,0:T(8,128)S(1)}, f32[256,8,64]{2,1,0:T(8,128)}, u32[]{:S(2)}) copy-start(f32[256,8,64]{2,1,0:T(8,128)} %copy.94) | copy-start | bytes 1572868
  233.9 8.2 %copy-start.9 = (f32[256,8,64]{2,1,0:T(8,128)S(1)}, f32[256,8,64]{2,1,0:T(8,128)}, u32[]{:S(2)}) copy-start(f32[256,8,64]{2,1,0:T(8,128)} %copy.93) | copy-start | bytes 1572868
  241.0 1.6 collective-permute-start.8
  241.3 1.6 collective-permute-start.10
  241.5 2.1 collective-permute-start.12
  241.8 25.4 %collective-permute-start.7 = (bf16[256,512]{0,1:T(8,128)(2,1)}, bf16[256,512]{0,1:T(8,128)(2,1)}, u32[]{:S(2)}, u32[]{:S(2)}) collective-permute-start(bf16[256,512]{0,1:T(8,128)(2,1)} %get-tuple-element.42), channel_id=1, source_target_pairs={{0,4},{4,0},{8,12},{12,8},{16,20},{20,16},{24,28},{28,24},{1,5},{5... | collective-permute-start | bytes 786440 | tf_op jit(solution)/shard_map/ppermute | solution.py:54
  244.6 23.9 %collective-permute-start.13 = (bf16[256,512]{0,1:T(8,128)(2,1)}, bf16[256,512]{0,1:T(8,128)(2,1)S(1)}, u32[]{:S(2)}, u32[]{:S(2)}) collective-permute-start(bf16[256,512]{0,1:T(8,128)(2,1)} %get-tuple-element.48), channel_id=1, source_target_pairs={{0,24},{4,28},{8,16},{12,20},{16,8},{20,12},{24,0},{28,4},{1,25},{... | collective-permute-start | bytes 786440 | tf_op jit(solution)/shard_map/ppermute | solution.py:54
  247.5 25.3 %collective-permute-start.11 = (bf16[256,512]{0,1:T(8,128)(2,1)}, bf16[256,512]{0,1:T(8,128)(2,1)}, u32[]{:S(2)}, u32[]{:S(2)}) collective-permute-start(bf16[256,512]{0,1:T(8,128)(2,1)} %get-tuple-element.47), channel_id=1, source_target_pairs={{0,16},{4,20},{8,24},{12,28},{16,0},{20,4},{24,8},{28,12},{1,17},{... | collective-permute-start | bytes 786440 | tf_op jit(solution)/shard_map/ppermute | solution.py:54
  248.0 24.8 %collective-permute-start.9 = (bf16[256,512]{0,1:T(8,128)(2,1)}, bf16[256,512]{0,1:T(8,128)(2,1)}, u32[]{:S(2)}, u32[]{:S(2)}) collective-permute-start(bf16[256,512]{0,1:T(8,128)(2,1)} %get-tuple-element.46), channel_id=1, source_target_pairs={{0,8},{4,12},{8,0},{12,4},{16,24},{20,28},{24,16},{28,20},{1,9},{5... | collective-permute-start | bytes 786440 | tf_op jit(solution)/shard_map/ppermute | solution.py:54
  274.9 6.7 %slice-start.4 = ((f32[256,512]{0,1:T(8,128)}), f32[256,256]{0,1:T(8,128)S(1)}, s32[]{:S(2)}) async-start(f32[256,512]{0,1:T(8,128)} %convert_add_fusion), calls=%async_computation.12 | async-start | bytes 524288 | tf_op jit(solution)/shard_map/slice | solution.py:171
  281.7 6.1 %copy-start.10 = (bf16[8192,256]{1,0:T(8,128)(2,1)S(1)}, bf16[8192,256]{1,0:T(8,128)(2,1)}, u32[]{:S(2)}) copy-start(bf16[8192,256]{1,0:T(8,128)(2,1)} %param.12) | copy-start | bytes 12582916
  281.7 6.1 %copy-start.11 = (f32[256,512]{0,1:T(8,128)S(1)}, f32[256,512]{0,1:T(8,128)}, u32[]{:S(2)}) copy-start(f32[256,512]{0,1:T(8,128)} %convert_add_fusion) | copy-start | bytes 1572868
  291.2 14.9 %collective-permute-start.14 = (bf16[256,1024]{0,1:T(8,128)(2,1)S(1)}, bf16[256,1024]{0,1:T(8,128)(2,1)S(1)}, u32[]{:S(2)}, u32[]{:S(2)}) collective-permute-start(bf16[256,1024]{0,1:T(8,128)(2,1)S(1)} %bitcast.129), channel_id=1, source_target_pairs={{0,8},{4,12},{8,0},{12,4},{16,24},{20,28},{24,16},{28,20},{1,9},{5... | collective-permute-start | bytes 1572872 | tf_op jit(solution)/shard_map/ppermute | solution.py:54
  292.7 24.8 %collective-permute-start.15 = (bf16[256,1024]{0,1:T(8,128)(2,1)S(1)}, bf16[256,1024]{0,1:T(8,128)(2,1)S(1)}, u32[]{:S(2)}, u32[]{:S(2)}) collective-permute-start(bf16[256,1024]{0,1:T(8,128)(2,1)S(1)} %bitcast.130), channel_id=1, source_target_pairs={{0,16},{4,20},{8,24},{12,28},{16,0},{20,4},{24,8},{28,12},{1,17},{... | collective-permute-start | bytes 1572872 | tf_op jit(solution)/shard_map/ppermute | solution.py:54
  293.4 24.2 %collective-permute-start.16 = (bf16[256,1024]{0,1:T(8,128)(2,1)S(1)}, bf16[256,1024]{0,1:T(8,128)(2,1)S(1)}, u32[]{:S(2)}, u32[]{:S(2)}) collective-permute-start(bf16[256,1024]{0,1:T(8,128)(2,1)S(1)} %bitcast.131), channel_id=1, source_target_pairs={{0,24},{4,28},{8,16},{12,20},{16,8},{20,12},{24,0},{28,4},{1,25},{... | collective-permute-start | bytes 1572872 | tf_op jit(solution)/shard_map/ppermute | solution.py:54
  294.8 23.6 %collective-permute-start.17 = (bf16[256,1024]{0,1:T(8,128)(2,1)S(1)}, bf16[256,1024]{0,1:T(8,128)(2,1)S(1)}, u32[]{:S(2)}, u32[]{:S(2)}) collective-permute-start(bf16[256,1024]{0,1:T(8,128)(2,1)S(1)} %bitcast.132), channel_id=1, source_target_pairs={{0,4},{4,0},{8,12},{12,8},{16,20},{20,16},{24,28},{28,24},{1,5},{5... | collective-permute-start | bytes 1572872 | tf_op jit(solution)/shard_map/ppermute | solution.py:54
  306.1 12.3 %collective-permute-start.18 = (bf16[256,1024]{0,1:T(8,128)(2,1)S(1)}, bf16[256,1024]{0,1:T(8,128)(2,1)S(1)}, u32[]{:S(2)}, u32[]{:S(2)}) collective-permute-start(bf16[256,1024]{0,1:T(8,128)(2,1)S(1)} %collective-permute-done.14), channel_id=1, source_target_pairs={{0,4},{4,0},{8,12},{12,8},{16,20},{20,16},{24,28},{28,24},{1,5},{5... | collective-permute-start | bytes 1572872 | tf_op jit(solution)/shard_map/ppermute | solution.py:54
  317.5 1.9 collective-permute-start.19
  317.6 2.6 collective-permute-start.20
  322.6 20.4 %collective-permute-start.21 = (bf16[256,1536]{1,0:T(8,128)(2,1)S(1)}, bf16[256,1536]{1,0:T(8,128)(2,1)S(1)}, u32[]{:S(2)}, u32[]{:S(2)}) collective-permute-start(bf16[256,1536]{1,0:T(8,128)(2,1)S(1)} %pad_maximum_fusion), channel_id=1, source_target_pairs={{0,8},{4,12},{8,0},{12,4},{16,24},{20,28},{24,16},{28,20},{1,9},{5... | collective-permute-start | bytes 2359304 | tf_op jit(solution)/shard_map/ppermute | solution.py:54
  323.0 36.2 %collective-permute-start.22 = (bf16[256,1536]{1,0:T(8,128)(2,1)S(1)}, bf16[256,1536]{1,0:T(8,128)(2,1)S(1)}, u32[]{:S(2)}, u32[]{:S(2)}) collective-permute-start(bf16[256,1536]{1,0:T(8,128)(2,1)S(1)} %pad_maximum_fusion), channel_id=1, source_target_pairs={{0,16},{4,20},{8,24},{12,28},{16,0},{20,4},{24,8},{28,12},{1,17},{... | collective-permute-start | bytes 2359304 | tf_op jit(solution)/shard_map/ppermute | solution.py:54
  323.6 35.6 %collective-permute-start.23 = (bf16[256,1536]{1,0:T(8,128)(2,1)S(1)}, bf16[256,1536]{1,0:T(8,128)(2,1)S(1)}, u32[]{:S(2)}, u32[]{:S(2)}) collective-permute-start(bf16[256,1536]{1,0:T(8,128)(2,1)S(1)} %pad_maximum_fusion), channel_id=1, source_target_pairs={{0,24},{4,28},{8,16},{12,20},{16,8},{20,12},{24,0},{28,4},{1,25},{... | collective-permute-start | bytes 2359304 | tf_op jit(solution)/shard_map/ppermute | solution.py:54
  326.1 33.7 %collective-permute-start.24 = (bf16[256,1536]{1,0:T(8,128)(2,1)S(1)}, bf16[256,1536]{1,0:T(8,128)(2,1)S(1)}, u32[]{:S(2)}, u32[]{:S(2)}) collective-permute-start(bf16[256,1536]{1,0:T(8,128)(2,1)S(1)} %pad_maximum_fusion), channel_id=1, source_target_pairs={{0,4},{4,0},{8,12},{12,8},{16,20},{20,16},{24,28},{28,24},{1,5},{5... | collective-permute-start | bytes 2359304 | tf_op jit(solution)/shard_map/ppermute | solution.py:54
  343.0 16.9 %collective-permute-start.25 = (bf16[256,1536]{1,0:T(8,128)(2,1)S(1)}, bf16[256,1536]{1,0:T(8,128)(2,1)S(1)}, u32[]{:S(2)}, u32[]{:S(2)}) collective-permute-start(bf16[256,1536]{1,0:T(8,128)(2,1)S(1)} %collective-permute-done.21), channel_id=1, source_target_pairs={{0,4},{4,0},{8,12},{12,8},{16,20},{20,16},{24,28},{28,24},{1,5},{5... | collective-permute-start | bytes 2359304 | tf_op jit(solution)/shard_map/ppermute | solution.py:54
  359.1 2.3 collective-permute-start.26
  359.2 3.3 collective-permute-start.27
  (6 other events, 18.4 us)
Sparse Core Ops, SparseCore 0:
  10.1 83.4 all-gather.2
  117.5 79.4 all-gather.4
  199.8 75.2 reduce-scatter.2
  291.4 74.4 reduce-scatter.4
